TPU v7x, 32 devices: a whole 2x2x4 slice. The times are simulated.
32 devices in a mesh: row: 8 (over z, x), col: 4 (over y, core).
Axes of the slice: x: 2, y: 2, z: 4, core: 2. Of those that a mesh axis runs over, the one named last changes fastest.
Arguments:
- left_factors: bfloat16 [32, 512, 2048], P(None, 'row', 'col'), may hold values from -0.890625 to 0.890625
- right_factors: bfloat16 [512, 131072], P('col', 'row'), may hold values from -0.890625 to 0.890625
- amplitudes: bfloat16 [512, 512, 256], P('row', 'col'), may hold values from -0.015625 to 0.015625
- eps_left: float32 [32], P('col'), may hold values from 0.2 to 1.5
- eps_right: float32 [64], replicated, may hold values from 0.2 to 1.5
- pair_energy: float32 [256], P('row'), may hold values from -2 to -0.5
Outputs:
- update: float32 [256, 32, 64], P('row', 'col')
All inputs are finite; a program needn't handle non-finite values.
Results may differ from a plain program's by a relative error of at most 0.0029.
Values may be sent and summed in bfloat16 or wider, within the bound.
No kernel may reach another device: no remote copies, remote signals or barrier semaphores. Data moves between devices by JAX's collectives and lax.ppermute only.
A program may use at most 128 MiB of HBM per device.

v0:
```python
import jax
import jax.numpy as jnp
from jax import lax
from jax.sharding import PartitionSpec as P


def contract_aux(left_piece, right_piece):
    return lax.dot_general(
        left_piece, right_piece, (((2,), (1,)), ((), ())), preferred_element_type=jnp.float32
    )


def per_device(left_factors, right_factors, amplitudes, eps_left, eps_right, pair_energy):
    width_a, local_c, _ = left_factors.shape
    local_d = right_factors.shape[0]
    width_b = eps_right.shape[0]
    pairs = amplitudes.shape[2]
    gathered = lax.all_gather(right_factors, "row", axis=1, tiled=True)
    right_whole = gathered.reshape(local_d, -1, width_b)
    left_whole = lax.all_gather(left_factors, "col", axis=2, tiled=True)
    integ = contract_aux(left_whole, right_whole)
    integ = integ.astype(jnp.bfloat16)
    n_row = lax.axis_size("row")
    n_col = lax.axis_size("col")
    own_pairs = pairs // n_row
    own_a = width_a // n_col
    partial_value = jnp.einsum(
        "cdp,acdb->pab", amplitudes, integ, preferred_element_type=jnp.float32
    )
    partial_value = partial_value.reshape(pairs, width_a * width_b)
    section = lax.psum_scatter(partial_value, "row", scatter_dimension=0, tiled=True)
    ladder = lax.psum_scatter(section, "col", scatter_dimension=1, tiled=True)
    ladder = ladder.reshape(own_pairs, own_a, width_b)
    denom = eps_left[None, :, None] + eps_right[None, None, :] - pair_energy[:, None, None]
    return ladder / denom


def solution(mesh):
    in_specs = (
        P(None, "row", "col"),
        P("col", "row"),
        P("row", "col", None),
        P("col"),
        P(),
        P("row"),
    )
    out_specs = P("row", "col", None)
    return jax.shard_map(
        per_device, mesh=mesh, in_specs=in_specs, out_specs=out_specs, check_vma=False
    )
```

profile of v0, /device:TPU:0, one launch (start us, length us, event | category | flops | bytes accessed | tf_op | source)
XLA Modules:
  0.0 926.3 jit_solution(1580056474967747443)
XLA Ops:
  6.5 0.0 all-gather.5.cloned.1.call-start
  6.5 6.4 copy.10
  12.9 0.0 all-gather.5.cloned.1.call-update
  13.0 0.0 all-gather.3.cloned.1.call-start
  13.0 0.7 all-gather.3.cloned.1.call-update
  13.7 0.0 reduce-scatter.7.cloned.1.call-start
  13.8 639.8 %all-gather.5.cloned.1.call-done = bf16[128,131072]{0,1:T(8,128)(2,1)} async-done(((bf16[128,16384]{0,1:T(8,128)(2,1)}), bf16[128,131072]{0,1:T(8,128)(2,1)}) %all-gather.5.cloned.1.call-update) | async-done | bytes 33554448 | tf_op jit(solution)/shard_map/all_gather | solution.py:18
  653.5 47.2 %copy.11 = bf16[128,2048,64]{1,0,2:T(8,128)(2,1)} copy(bf16[128,2048,64]{0,2,1:T(8,128)(2,1)} %bitcast.22) | data formatting | bytes 67108864 | tf_op jit(solution)/shard_map/reshape | solution.py:19
  700.8 12.6 %all-gather.3.cloned.1.call-done = bf16[32,64,2048]{2,1,0:T(8,128)(2,1)} async-done(((bf16[32,64,512]{2,1,0:T(8,128)(2,1)}), bf16[32,64,2048]{2,1,0:T(8,128)(2,1)}) %all-gather.3.cloned.1.call-update) | async-done | bytes 8388624 | tf_op jit(solution)/shard_map/all_gather | solution.py:20
  713.4 0.0 copy-start.3
  713.4 78.3 %fusion.4 = bf16[32,64,128,64]{2,1,3,0:T(8,128)(2,1)} fusion(bf16[128,2048,64]{1,0,2:T(8,128)(2,1)} %copy.11, bf16[32,64,2048]{2,1,0:T(8,128)(2,1)} %all-gather.3.cloned.1.call-done), kind=kOutput, calls=%fused_computation.4 | convolution fusion | flops 68736253952 | bytes 75497472 | tf_op jit(solution)/shard_map/dot_general | solution.py:8
  791.7 0.0 copy-done.3
  791.7 30.0 %fusion.2 = f32[32,64,256,1]{2,1,3,0:T(8,128)S(1)} fusion(bf16[32,64,128,64]{2,1,3,0:T(8,128)(2,1)} %fusion.4, bf16[64,128,256]{2,1,0:T(8,128)(2,1)S(1)} %copy-done.3), kind=kOutput, calls=%fused_computation.2 | convolution fusion | flops 8589934592 | bytes 39845888 | tf_op jit(solution)/shard_map/cdp,acdb->pab/dot_general | solution.py:27
  821.6 0.0 copy-start.1
  821.6 0.0 copy-start.2
  821.7 0.0 copy-start
  821.7 1.9 copy.16
  823.5 0.0 reduce-scatter.7.cloned.1.call-update
  823.6 0.0 reduce-scatter.5.cloned.1.call-start
  823.6 67.9 %reduce-scatter.7.cloned.1.call-done = f32[32,2048]{1,0:T(8,128)} async-done(((f32[256,2048]{1,0:T(8,128)}), f32[32,2048]{1,0:T(8,128)}) %reduce-scatter.7.cloned.1.call-update) | async-done | bytes 262160
  891.5 2.3 copy.17
  893.7 0.0 reduce-scatter.5.cloned.1.call-update
  893.8 0.0 copy-done.1
  893.8 0.0 copy-done.2
  893.8 0.1 broadcast_add_fusion
  893.9 24.0 %reduce-scatter.5.cloned.1.call-done = f32[32,512]{0,1:T(8,128)} async-done(((f32[32,2048]{0,1:T(8,128)}), f32[32,512]{0,1:T(8,128)}) %reduce-scatter.5.cloned.1.call-update) | async-done | bytes 65552 | tf_op jit(solution)/shard_map/reduce_scatter | solution.py:32
  917.9 1.1 copy.13
  919.0 0.0 copy-done
  919.0 0.8 subtract_divide_fusion
Async XLA Ops:
  6.5 647.0 %all-gather.5.cloned.1.call-start = ((), (), s32[]{:S(2)}) async-start(), calls=%async_computation.3 | async-start | bytes 37748736 | tf_op jit(solution)/shard_map/all_gather | solution.py:18
  13.0 700.4 %all-gather.3.cloned.1.call-start = ((), (), s32[]{:S(2)}) async-start(), calls=%async_computation.2 | async-start | bytes 10485760 | tf_op jit(solution)/shard_map/all_gather | solution.py:20
  13.7 877.8 %reduce-scatter.7.cloned.1.call-start = ((), (), s32[]{:S(2)}) async-start(), calls=%async_computation.5 | async-start | bytes 2359296
  713.4 78.3 %copy-start.3 = (bf16[64,128,256]{2,1,0:T(8,128)(2,1)S(1)}, bf16[64,128,256]{2,1,0:T(8,128)(2,1)}, u32[]{:S(2)}) copy-start(bf16[64,128,256]{2,1,0:T(8,128)(2,1)} %param.8) | copy-start | bytes 12582916
  821.6 72.1 %copy-start.1 = (f32[64]{0:T(128)S(1)}, f32[64]{0:T(128)}, u32[]{:S(2)}) copy-start(f32[64]{0:T(128)} %param.10) | copy-start | bytes 772
  821.6 72.1 %copy-start.2 = (f32[8]{0:T(128)S(1)}, f32[8]{0:T(128)}, u32[]{:S(2)}) copy-start(f32[8]{0:T(128)} %param.9) | copy-start | bytes 100
  821.7 97.3 %copy-start = (f32[32]{0:T(128)S(1)}, f32[32]{0:T(128)}, u32[]{:S(2)}) copy-start(f32[32]{0:T(128)} %param.11) | copy-start | bytes 388
  823.6 94.3 %reduce-scatter.5.cloned.1.call-start = ((), (), s32[]{:S(2)}) async-start(), calls=%async_computation.4 | async-start | bytes 1310720 | tf_op jit(solution)/shard_map/reduce_scatter | solution.py:32
Sparse Core Ops, SparseCore 0:
  13.1 640.4 all-gather.4
  655.1 58.2 all-gather.2
  823.7 67.7 reduce-scatter.6
  893.9 23.9 reduce-scatter.4
where the time goes:
time: 928 us; the launch traced here: 926 us
  waiting for transfers between devices  745 us (80%)
  matrix products  108 us (12%)
  local copies, waits for them, and re-layouts  58.9 us (6%)
  between operations  13.2 us (1%)
    all_gather x1, waiting for transfers between devices, per_device(): gathered = lax.all_gather(right_factors, 'row', axis=1, tiled=True)  640 us
    dot_general x1, matrix products, contract_aux(): lax.dot_general(left_piece, right_piece, (((2,), (1,)), ((), ())), prefer...  78.3 us
    unnamed x5, waiting for transfers between devices  68.6 us
    reshape x1, local copies, waits for them, and re-layouts, per_device(): right_whole = gathered.reshape(local_d, -1, width_b)  47.2 us
    dot_general x1, matrix products, per_device(): jnp.einsum('cdp,acdb->pab', amplitudes, integ, preferred_element_type=jnp...  30 us
    reduce_scatter x1, waiting for transfers between devices, per_device(): ladder = lax.psum_scatter(section, 'col', scatter_dimension=1, tiled=True)  24 us
  transfers between devices with their start and end apart: 4, of which 4 were waited for; matrix products, arithmetic and copies ran while one was open for 5% of the time, Pallas kernels for 0%

commit v1 on v0

--- a/solution.py
+++ b/solution.py
@@ -1,7 +1,15 @@
+import functools
+
 import jax
 import jax.numpy as jnp
 from jax import lax
+from jax.experimental import pallas as pl
+from jax.experimental.pallas import tpu as pltpu
 from jax.sharding import PartitionSpec as P
+
+AXES = ("row", "col")
+CHUNKS = 4
+SPLIT = 2
 
 
 def contract_aux(left_piece, right_piece):
@@ -10,7 +18,7 @@
     )
 
 
-def per_device(left_factors, right_factors, amplitudes, eps_left, eps_right, pair_energy):
+def gathered_whole(left_factors, right_factors, amplitudes, eps_left, eps_right, pair_energy):
     width_a, local_c, _ = left_factors.shape
     local_d = right_factors.shape[0]
     width_b = eps_right.shape[0]
@@ -35,7 +43,215 @@
     return ladder / denom
 
 
+def ladder_kernel(slots, which_ref, *refs):
+    pieces = refs[:slots]
+    left_ref, amp_own_ref, amp_other_ref, add_ref, out_ref = refs[slots:]
+    depth, width_b, width_q = pieces[0].shape
+    tile_a, _, chunk_c, _ = left_ref.shape[2:]
+    span = 2 * chunk_c
+    integ = None
+    for s in range(slots):
+        left = left_ref[which_ref[2 * s], which_ref[2 * s + 1]].reshape(tile_a * span, width_q)
+        right = pieces[s][...].reshape(depth * width_b, width_q)
+        term = lax.dot_general(
+            right, left, (((1,), (1,)), ((), ())), preferred_element_type=jnp.float32
+        )
+        integ = term if integ is None else integ + term
+    integ = integ.astype(jnp.bfloat16)
+    integ = jnp.concatenate(
+        [
+            jnp.concatenate(
+                [
+                    integ[d * width_b : (d + 1) * width_b, a * span : (a + 1) * span]
+                    for d in range(depth)
+                ],
+                axis=1,
+            )
+            for a in range(tile_a)
+        ],
+        axis=0,
+    )
+    amp = jnp.concatenate([amp_own_ref[...], amp_other_ref[...]], axis=1)
+    amp = amp.reshape(depth * span, -1)
+    out = jnp.dot(integ, amp, preferred_element_type=jnp.float32)
+    out_ref[...] = add_ref[...] + out.reshape(out_ref.shape)
+
+
+def add_ladder(pieces, which, left, amp_own, amp_other, add, tile_a=4):
+    slots = len(pieces)
+    depth, width_b, width_q = pieces[0].shape
+    width_a, _, chunk_c, _ = left.shape[2:]
+    pairs = amp_own.shape[-1]
+
+    def whole(array):
+        return pl.BlockSpec(array.shape, lambda i, w: (0,) * array.ndim)
+
+    left_spec = pl.BlockSpec(
+        left.shape[:2] + (tile_a,) + left.shape[3:], lambda i, w: (0, 0, i, 0, 0, 0)
+    )
+    out_spec = pl.BlockSpec((tile_a, width_b, pairs), lambda i, w: (i, 0, 0))
+    products = depth * width_b * width_a * 2 * chunk_c * (slots * width_q + pairs)
+    moved = sum(2 * v.size for v in (*pieces, left, amp_own, amp_other)) + 8 * add.size
+    return pl.pallas_call(
+        functools.partial(ladder_kernel, slots),
+        grid_spec=pltpu.PrefetchScalarGridSpec(
+            num_scalar_prefetch=1,
+            grid=(width_a // tile_a,),
+            in_specs=[whole(v) for v in pieces]
+            + [left_spec, whole(amp_own), whole(amp_other), out_spec],
+            out_specs=out_spec,
+        ),
+        out_shape=jax.ShapeDtypeStruct(add.shape, jnp.float32),
+        input_output_aliases={slots + 4: 0},
+        cost_estimate=pl.CostEstimate(flops=2 * products, bytes_accessed=moved, transcendentals=0),
+        compiler_params=pltpu.CompilerParams(vmem_limit_bytes=52 * 2**20),
+        name="ladder",
+    )(which, *pieces, left, amp_own, amp_other, add)
+
+
+def by_lines(n_row, n_col, *arrays):
+    left_factors, right_factors, amplitudes, eps_left, eps_right, pair_energy = arrays
+    row, col = lax.axis_index("row"), lax.axis_index("col")
+    n_z, n_y = n_row // 2, n_col // 2
+    z, x, y, core = row // 2, row % 2, col // 2, col % 2
+    half = n_z // 2
+
+    def inner(at):
+        return at in (half - 1, half)
+
+    def send(value, place):
+        pairs = []
+        for at_z in range(n_z):
+            for at_x in range(2):
+                for at_y in range(n_y):
+                    for at_k in range(2):
+                        to = place(at_z, at_x, at_y, at_k)
+                        if to is not None:
+                            source = (at_z * 2 + at_x) * n_col + at_y * 2 + at_k
+                            target = (to[0] * 2 + to[1]) * n_col + to[2] * 2 + to[3]
+                            pairs.append((source, target))
+        return lax.ppermute(value, AXES, pairs)
+
+    def other_x(c, x, y, k):
+        return c, 1 - x, y, k
+
+    def other_y(c, x, y, k):
+        return c, x, 1 - y, k
+
+    def other_core(c, x, y, k):
+        return c, x, y, 1 - k
+
+    def near(c, x, y, k):
+        return c ^ 1, x, y, k
+
+    def across(c, x, y, k):
+        return (n_z - 1 - c, x, y, k) if inner(c) else None
+
+    def outward(c, x, y, k):
+        return (c ^ 1, x, y, k) if inner(c) else None
+
+    def inward(c, x, y, k):
+        return None if inner(c) else (c ^ 1, x, y, k)
+
+    def far_y(c):
+        return 1 - c // half
+
+    is_inner = (z == half - 1) | (z == half)
+
+    def pick(value, at):
+        return lax.dynamic_index_in_dim(value, at, 0, keepdims=False)
+
+    local_d = right_factors.shape[0]
+    width_b = eps_right.shape[0]
+    depth = local_d // 2 // CHUNKS
+    right = right_factors.reshape(2, CHUNKS, depth, -1, width_b)
+    chunks = range(CHUNKS)
+    right_keep, right_give = pick(right, x), pick(right, 1 - x)
+    give = [right_give[i].transpose(0, 2, 1) for i in chunks]
+    own = [right_keep[i].transpose(0, 2, 1) for i in chunks]
+    far = [send(v, other_x) for v in give]
+    blocks = []
+    for i in chunks:
+        zero = (own[i], far[i])
+        one = tuple(send(v, near) for v in zero)
+        two = tuple(send(v, across) for v in zero)
+        three = tuple(send(v, across) for v in one)
+        if i < CHUNKS - SPLIT:
+            two, three = (
+                tuple(jnp.where(is_inner, v, send(v, outward)) for v in pair)
+                for pair in (two, three)
+            )
+        blocks.append((*zero, *one, *two, *three))
+
+    local_c, _, pairs = amplitudes.shape
+    amp = amplitudes.reshape(local_c, 2, CHUNKS, depth, pairs)
+    amp_keep = lax.dynamic_index_in_dim(amp, x, 1, keepdims=False)
+    amp_give = lax.dynamic_index_in_dim(amp, 1 - x, 1, keepdims=False)
+    amp_own = [amp_keep[:, i].transpose(1, 0, 2) for i in chunks]
+    amp_far = [send(amp_give[:, i].transpose(1, 0, 2), other_x) for i in chunks]
+
+    width_a, _, local_q = left_factors.shape
+    mine = left_factors.reshape(width_a, local_c, 2, local_q // 2).transpose(2, 0, 1, 3)
+    mine_x = send(mine, other_x)
+    here = jnp.stack([mine, mine_x], axis=2)
+    here_y = jnp.stack([send(mine, other_y), send(mine_x, other_y)], axis=2)
+    left = jnp.stack([here, send(here, other_core), here_y, send(here_y, other_core)])
+
+    def in_far(c, x, y, k):
+        return (c ^ 1, x, y, k) if not inner(c) and y == far_y(c) else None
+
+    def far_x(c, x, y, k):
+        return (c, 1 - x, y, k) if inner(c) and y == far_y(c) else None
+
+    def far_to_y(c, x, y, k):
+        return (c, x, 1 - y, k) if inner(c) and y == far_y(c) else None
+
+    got = send(mine, in_far)
+    got_x = send(got, far_x)
+    got, got_x = (jnp.where(y == far_y(z), v, send(v, far_to_y)) for v in (got, got_x))
+    end = jnp.stack([got, got_x], axis=2)
+    end = jnp.stack([end, send(end, other_core)])
+
+    far_inner = jnp.where(z < half, half, half - 1)
+    planes = (z, z ^ 1, far_inner, far_inner ^ 1)
+    which = jnp.stack([v for p in planes for v in (p ^ col, x, p ^ col, 1 - x)])
+    which_end = jnp.stack([v for p in planes[2:] for v in ((p % 2) ^ core, x, (p % 2) ^ core, 1 - x)])
+    total = jnp.zeros((width_a, width_b, pairs), jnp.float32)
+    for i in chunks:
+        total = add_ladder(blocks[i], which, left, amp_own[i], amp_far[i], total)
+        if i >= CHUNKS - SPLIT:
+            amp_end = [send(v, inward) for v in (amp_own[i], amp_far[i])]
+            total = add_ladder(blocks[i][4:], which_end, end, *amp_end, total)
+
+    own_a, own_pairs = width_a // n_col, pairs // n_row
+    total = total.reshape(n_y, 2, own_a, width_b, pairs)
+    keep = lax.dynamic_index_in_dim(total, core, 1, keepdims=False)
+    give = lax.dynamic_index_in_dim(total, 1 - core, 1, keepdims=False)
+    part = keep + send(give, other_core)
+    part = part.reshape(n_y, own_a * width_b, n_z, 2, own_pairs).transpose(3, 0, 2, 4, 1)
+
+    def over_x(v):
+        return pick(v, x) + send(pick(v, 1 - x), other_x)
+
+    def over_y(v):
+        return pick(v, y) + send(pick(v, 1 - y), other_y)
+
+    cut = own_pairs // 2
+    first = over_y(over_x(part[:, :, :, :cut]))
+    second = over_x(over_y(part[:, :, :, cut:].transpose(1, 0, 2, 3, 4)))
+    part = jnp.concatenate([first, second], axis=1)
+    ladder = pick(part, z)
+    for step in range(1, n_z):
+        ladder = ladder + send(pick(part, z ^ step), lambda c, x, y, k, s=step: (c ^ s, x, y, k))
+    ladder = ladder.reshape(own_pairs, own_a, width_b)
+    denom = eps_left[None, :, None] + eps_right[None, None, :] - pair_energy[:, None, None]
+    return ladder / denom
+
+
 def solution(mesh):
+    n_row, n_col = mesh.shape["row"], mesh.shape["col"]
+    lines = n_row == 2 * n_col and n_col == 4
+    per_device = functools.partial(by_lines, n_row, n_col) if lines else gathered_whole
     in_specs = (
         P(None, "row", "col"),
         P("col", "row"),

time: 928 us -> 576 us (0.62)
  waiting for transfers between devices: 745 us -> 160 us
  starting transfers between devices: 0.12 us -> 160 us
  Pallas kernels: 0 us -> 151 us
  matrix products: 108 us -> 0 us
  other arithmetic: 0.84 us -> 38.6 us
  between operations: 13.2 us -> 1.08 us
    all_gather x2 -> x0, waiting for transfers between devices: 652 us -> none  [the longest x1 640 us: per_device(): gathered = lax.all_gather(right_factors, 'row', axis=1, tiled=True)]
    ppermute x0 -> x62, starting transfers between devices: none -> 160 us  [send(): return lax.ppermute(value, AXES, pairs)]
    ppermute x0 -> x62, waiting for transfers between devices: none -> 160 us  [send(): return lax.ppermute(value, AXES, pairs)]
    pallas_call x0 -> x6, Pallas kernels: none -> 151 us  [add_ladder(): pl.pallas_call(functools.partial(ladder_kernel, slots), grid_spec=pltpu.P...]
    dot_general x2 -> x0, matrix products: 108 us -> none  [the longest x1 78.3 us: contract_aux(): lax.dot_general(left_piece, right_piece, (((2,), (1,)), ((), ())), prefer...]
    unnamed x5 -> x0, waiting for transfers between devices: 68.6 us -> none
    reshape x2 -> x4, local copies, waits for them, and re-layouts: 48.3 us -> 15.1 us  [the longest x1 11.3 us: by_lines(): right = right_factors.reshape(2, CHUNKS, depth, -1, width_b)]
    another operation x0 -> x7, other arithmetic: none -> 28.3 us  [the longest x3 15.7 us: by_lines(): jnp.stack([here, send(here, other_core), here_y, send(here_y, other_core)])]
  transfers between devices with their start and end apart: 4 -> 62, of which waited for: 4 -> 20; matrix products, arithmetic and copies ran while one was open for 5% -> 15% of each run, Pallas kernels for 0% -> 23%
where the time goes in v1:
time: 576 us; the launch traced here: 574 us
  starting transfers between devices  160 us (28%)
  waiting for transfers between devices  160 us (28%)
  Pallas kernels  151 us (26%)
  local copies, waits for them, and re-layouts  63.7 us (11%)
  other arithmetic  38.6 us (7%)
    ppermute x62, starting transfers between devices, send(): return lax.ppermute(value, AXES, pairs)  160 us
    ppermute x62, waiting for transfers between devices, send(): return lax.ppermute(value, AXES, pairs)  160 us
    pallas_call x6, Pallas kernels, add_ladder(): pl.pallas_call(functools.partial(ladder_kernel, slots), grid_spec=pltpu.P...  151 us
    unnamed x114, local copies, waits for them, and re-layouts  21.8 us
    another operation x3, other arithmetic, by_lines(): jnp.stack([here, send(here, other_core), here_y, send(here_y, other_core)])  15.7 us
    another operation x2, other arithmetic, by_lines(): end = jnp.stack([end, send(end, other_core)])  12.1 us
  transfers between devices with their start and end apart: 62, of which 20 were waited for; matrix products, arithmetic and copies ran while one was open for 15% of the time, Pallas kernels for 23%

profile of v1, /device:TPU:0, one launch (start us, length us, event | category | flops | bytes accessed | tf_op | source)
XLA Modules:
  0.0 574.1 jit_solution(2956160795617810392)
XLA Ops:
  0.0 3.2 copy.66
  3.2 2.9 collective-permute-start.15
  6.1 11.3 %reshape.71 = bf16[2,4,16,256,64]{4,3,2,1,0:T(8,128)(2,1)} reshape(bf16[128,16384]{1,0:T(8,128)(2,1)} %param.7) | data formatting | bytes 8388608 | tf_op jit(solution)/shard_map/reshape | solution.py:167
  17.5 6.4 %constant_dynamic-slice_fusion.10 = (bf16[1,1,16,256,64]{4,3,2,1,0:T(8,128)(2,1)S(1)}, bf16[1,1,16,256,64]{4,3,2,1,0:T(8,128)(2,1)}, bf16[1,1,16,256,64]{4,3,2,1...) fusion(bf16[2,4,16,256,64]{4,3,2,1,0:T(8,128)(2,1)} %reshape.71, ...), kind=kLoop, calls=%fused_computation.67 | loop fusion | bytes 8388628 | tf_op jit(solution)/shard_map/slice | solution.py:170
  26.6 2.2 collective-permute-start.43
  30.2 2.0 collective-permute-start.7
  32.2 2.3 copy.56
  34.9 28.3 %collective-permute-done.42.refs_1_ = bf16[16,64,256]{2,1,0:T(8,128)(2,1)S(1)} collective-permute-done((bf16[16,64,256]{2,1,0:T(8,128)(2,1)}, bf16[16,64,256]{2,1,0:T(8,128)(2,1)S(1)}, u32[]{:S(2)}, u32[]{:S(2)}) %collective-permute-start.42) | collective-permute-done | bytes 524320 | tf_op jit(solution)/shard_map/ppermute | solution.py:133
  68.6 8.0 %collective-permute-done.30.refs_1_ = bf16[16,64,256]{2,1,0:T(8,128)(2,1)S(1)} collective-permute-done((bf16[16,64,256]{2,1,0:T(8,128)(2,1)}, bf16[16,64,256]{2,1,0:T(8,128)(2,1)S(1)}, u32[]{:S(2)}, u32[]{:S(2)}) %collective-permute-start.30) | collective-permute-done | bytes 524320 | tf_op jit(solution)/shard_map/ppermute | solution.py:133
  77.5 4.2 collective-permute-start.44
  83.2 8.7 %collective-permute-done.44.refs_3_ = bf16[16,64,256]{2,1,0:T(8,128)(2,1)} collective-permute-done((bf16[16,64,256]{2,1,0:T(8,128)(2,1)S(1)}, bf16[16,64,256]{2,1,0:T(8,128)(2,1)}, u32[]{:S(2)}, u32[]{:S(2)}) %collective-permute-start.44) | collective-permute-done | bytes 524320 | tf_op jit(solution)/shard_map/ppermute | solution.py:133
  93.9 29.4 %collective-permute-start.32 = (bf16[16,64,256]{2,1,0:T(8,128)(2,1)S(1)}, bf16[16,64,256]{2,1,0:T(8,128)(2,1)S(1)}, u32[]{:S(2)}, u32[]{:S(2)}) collective-permute-start(bf16[16,64,256]{2,1,0:T(8,128)(2,1)S(1)} %collective-permute-done.30.refs_1_), channel_id=1, source_target_pairs={{0,8},{1,9},{2,10},{3,11},{4,12},{5,13},{6,14},{7,15},{8,0},{9,1},... | collective-permute-start | bytes 1572872 | tf_op jit(solution)/shard_map/ppermute | solution.py:133
  123.3 2.0 collective-permute-start.9
  125.3 2.7 collective-permute-done.46
  128.7 7.0 %collective-permute-done.32.refs_3_ = bf16[16,64,256]{2,1,0:T(8,128)(2,1)S(1)} collective-permute-done((bf16[16,64,256]{2,1,0:T(8,128)(2,1)S(1)}, bf16[16,64,256]{2,1,0:T(8,128)(2,1)S(1)}, u32[]{:S(2)}, u32[]{:S(2)}) %collective-permute-start.32) | collective-permute-done | bytes 524320 | tf_op jit(solution)/shard_map/ppermute | solution.py:133
  137.8 19.9 %collective-permute-done.18 = bf16[2,32,64,256]{3,2,1,0:T(8,128)(2,1)S(1)} collective-permute-done((bf16[2,32,64,256]{3,2,1,0:T(8,128)(2,1)}, bf16[2,32,64,256]{3,2,1,0:T(8,128)(2,1)S(1)}, u32[]{:S(2)}, u32[]{:S(2)}) %collective-permute-start.18) | collective-permute-done | bytes 2097184 | tf_op jit(solution)/shard_map/ppermute | solution.py:133
  159.1 5.2 fusion.12
  164.3 4.1 fusion.11
  170.7 2.3 constant_dynamic-slice_fusion.8
  175.7 2.3 copy.50
  181.1 4.7 copy_bitcast_fusion
  187.7 10.5 %collective-permute-done.48 = bf16[16,64,256]{2,1,0:T(8,128)(2,1)S(1)} collective-permute-done((bf16[16,64,256]{2,1,0:T(8,128)(2,1)}, bf16[16,64,256]{2,1,0:T(8,128)(2,1)S(1)}, u32[]{:S(2)}, u32[]{:S(2)}) %collective-permute-start.48) | collective-permute-done | bytes 524320 | tf_op jit(solution)/shard_map/ppermute | solution.py:133
  202.6 11.1 %collective-permute-done.38 = bf16[16,64,256]{2,1,0:T(8,128)(2,1)S(1)} collective-permute-done((bf16[16,64,256]{2,1,0:T(8,128)(2,1)S(1)}, bf16[16,64,256]{2,1,0:T(8,128)(2,1)S(1)}, u32[]{:S(2)}, u32[]{:S(2)}) %collective-permute-start.38) | collective-permute-done | bytes 524320 | tf_op jit(solution)/shard_map/ppermute | solution.py:133
  216.7 1.9 broadcast_select_fusion.1.refs_6_
  218.6 9.8 %collective-permute-done.36 = bf16[16,64,256]{2,1,0:T(8,128)(2,1)S(1)} collective-permute-done((bf16[16,64,256]{2,1,0:T(8,128)(2,1)S(1)}, bf16[16,64,256]{2,1,0:T(8,128)(2,1)S(1)}, u32[]{:S(2)}, u32[]{:S(2)}) %collective-permute-start.36) | collective-permute-done | bytes 524320 | tf_op jit(solution)/shard_map/ppermute | solution.py:133
  231.4 11.0 %collective-permute-done.52 = bf16[16,64,256]{2,1,0:T(8,128)(2,1)S(1)} collective-permute-done((bf16[16,64,256]{2,1,0:T(8,128)(2,1)}, bf16[16,64,256]{2,1,0:T(8,128)(2,1)S(1)}, u32[]{:S(2)}, u32[]{:S(2)}) %collective-permute-start.52) | collective-permute-done | bytes 524320 | tf_op jit(solution)/shard_map/ppermute | solution.py:133
  245.6 10.8 %collective-permute-done.40 = bf16[16,64,256]{2,1,0:T(8,128)(2,1)S(1)} collective-permute-done((bf16[16,64,256]{2,1,0:T(8,128)(2,1)S(1)}, bf16[16,64,256]{2,1,0:T(8,128)(2,1)S(1)}, u32[]{:S(2)}, u32[]{:S(2)}) %collective-permute-start.40) | collective-permute-done | bytes 524320 | tf_op jit(solution)/shard_map/ppermute | solution.py:133
  259.0 4.4 fusion.13
  265.5 6.4 %pad_maximum_fusion = bf16[4,2,32,2,64,256]{5,4,2,1,3,0:T(8,128)(2,1)S(1)} fusion(bf16[1,2,32,2,64,256]{5,4,2,1,3,0:T(8,128)(2,1)} %bitcast.33, bf16[1,2,32,2,64,256]{5,4,2,1,3,0:T(8,128)(2,1)S(1)} %copy-done.17, bf16[1,2,32,2,64,256]{5,4,2,1,3,0:T(8,128)(2,1)} %bitcast.29, bf16[1,2,32,2,64,256]{5,4,2,1,3,0:T(8,128)(2,1)S(1)} %copy-done.16), kind=kLoop, calls=%fused_computation | loop fusion | flops 25165824 | bytes 33554432 | tf_op jit(solution)/shard_map/stack | solution.py:198
  271.9 6.7 %copy.43.refs_8_ = bf16[4,2,32,2,64,256]{5,4,3,2,1,0:T(8,128)(2,1)} copy(bf16[4,2,32,2,64,256]{5,4,2,1,3,0:T(8,128)(2,1)S(1)} %pad_maximum_fusion) | data formatting | bytes 33554432 | tf_op jit(solution)/shard_map/stack | solution.py:198
  280.9 14.3 %collective-permute-done.21.refs_1_ = bf16[16,64,256]{2,1,0:T(8,128)(2,1)S(1)} collective-permute-done((bf16[16,64,256]{2,1,0:T(8,128)(2,1)S(1)}, bf16[16,64,256]{2,1,0:T(8,128)(2,1)S(1)}, u32[]{:S(2)}, u32[]{:S(2)}) %collective-permute-start.21) | collective-permute-done | bytes 524320 | tf_op jit(solution)/shard_map/ppermute | solution.py:133
  295.2 42.5 %collective-permute-start.25 = (bf16[16,64,256]{2,1,0:T(8,128)(2,1)S(1)}, bf16[16,64,256]{2,1,0:T(8,128)(2,1)S(1)}, u32[]{:S(2)}, u32[]{:S(2)}) collective-permute-start(bf16[16,64,256]{2,1,0:T(8,128)(2,1)S(1)} %collective-permute-done.21.refs_1_), channel_id=1, source_target_pairs={{0,8},{1,9},{2,10},{3,11},{4,12},{5,13},{6,14},{7,15},{8,0},{9,1},... | collective-permute-start | bytes 1572872 | tf_op jit(solution)/shard_map/ppermute | solution.py:133
  340.1 28.4 %ladder.6.refs_11_ = f32[32,64,256]{2,1,0:T(8,128)} custom-call(s32[16]{0:T(128)S(1)} %stack.112.which_ref, bf16[16,64,256]{2,1,0:T(8,128)(2,1)S(1)} %bitcast.144, bf16[16,64,256]{2,1,0:T(8,128)(2,1)S(1)} %copy-done.1, bf16[16,64,256]{2,1,0:T(8,128)(2,1)S(1)} %copy-done.3, ...), custom_call_target="tpu_custom_call", output_to_operand_aliasing={{}: (12, {})} | custom-call | flops 19327352832 | bytes 26214400 | tf_op jit(solution)/shard_map/ladder/pallas_call | solution.py:95
  372.1 28.4 %ladder.7.refs_11_ = f32[32,64,256]{2,1,0:T(8,128)} custom-call(s32[16]{0:T(128)S(1)} %stack.112.which_ref, bf16[16,64,256]{2,1,0:T(8,128)(2,1)S(1)} %bitcast.141, bf16[16,64,256]{2,1,0:T(8,128)(2,1)S(1)} %collective-permute-done.30.refs_1_, bf16[16,64,256]{2,1,0:T(8,128)(2,1)S(1)} %collective-permute-done.31.refs_2_, ...), custom_call_target="tpu_custom_call", output_to_operand_aliasing={{}: (12, {})} | custom-call | flops 19327352832 | bytes 26214400 | tf_op jit(solution)/shard_map/ladder/pallas_call | solution.py:95
  400.5 6.9 %collective-permute-start.27 = (bf16[16,64,256]{2,1,0:T(8,128)(2,1)S(1)}, bf16[16,64,256]{2,1,0:T(8,128)(2,1)S(1)}, u32[]{:S(2)}, u32[]{:S(2)}) collective-permute-start(bf16[16,64,256]{2,1,0:T(8,128)(2,1)S(1)} %copy-done.38), channel_id=1, source_target_pairs={{0,8},{1,9},{2,10},{3,11},{4,12},{5,13},{6,14},{7,15},{24,16},{25,... | collective-permute-start | bytes 1572872 | tf_op jit(solution)/shard_map/ppermute | solution.py:133
  407.5 4.7 collective-permute-start.29
  412.2 28.4 %ladder.8.refs_7_ = f32[32,64,256]{2,1,0:T(8,128)} custom-call(s32[16]{0:T(128)S(1)} %stack.112.which_ref, bf16[16,64,256]{2,1,0:T(8,128)(2,1)S(1)} %bitcast.150, bf16[16,64,256]{2,1,0:T(8,128)(2,1)S(1)} %collective-permute-done.21.refs_1_, bf16[16,64,256]{2,1,0:T(8,128)(2,1)S(1)} %collective-permute-done.23.refs_2_, ...), custom_call_target="tpu_custom_call", output_to_operand_aliasing={{}: (12, {})} | custom-call | flops 19327352832 | bytes 26214400 | tf_op jit(solution)/shard_map/ladder/pallas_call | solution.py:95
  442.6 7.7 %pad_maximum_fusion.1.refs_4_ = bf16[2,2,32,2,64,256]{5,4,3,2,1,0:T(8,128)(2,1)} fusion(bf16[1,2,32,2,64,256]{5,4,3,2,1,0:T(8,128)(2,1)} %bitcast.155, bf16[1,2,32,2,64,256]{5,4,3,2,1,0:T(8,128)(2,1)} %get-tuple-element.19), kind=kLoop, calls=%fused_computation.1 | loop fusion | flops 4194304 | bytes 16777216 | tf_op jit(solution)/shard_map/stack | solution.py:213
  454.3 18.8 %ladder.9.refs_11_ = f32[32,64,256]{2,1,0:T(8,128)} custom-call(s32[8]{0:T(128)S(1)} %stack.101.which_ref, bf16[16,64,256]{2,1,0:T(8,128)(2,1)S(1)} %copy-done.5, bf16[16,64,256]{2,1,0:T(8,128)(2,1)S(1)} %copy-done.7, bf16[16,64,256]{2,1,0:T(8,128)(2,1)S(1)} %copy-done.9, ...), custom_call_target="tpu_custom_call", output_to_operand_aliasing={{}: (8, {})} | custom-call | flops 10737418240 | bytes 15728640 | tf_op jit(solution)/shard_map/ladder/pallas_call | solution.py:95
  473.1 11.6 %collective-permute-start.12 = (bf16[16,64,256]{2,1,0:T(8,128)(2,1)S(1)}, bf16[16,64,256]{2,1,0:T(8,128)(2,1)S(1)}, u32[]{:S(2)}, u32[]{:S(2)}) collective-permute-start(bf16[16,64,256]{2,1,0:T(8,128)(2,1)S(1)} %copy-done.36), channel_id=1, source_target_pairs={{0,8},{1,9},{2,10},{3,11},{4,12},{5,13},{6,14},{7,15},{24,16},{25,... | collective-permute-start | bytes 1572872 | tf_op jit(solution)/shard_map/ppermute | solution.py:133
  487.9 28.4 %ladder.10.refs_7_ = f32[32,64,256]{2,1,0:T(8,128)} custom-call(s32[16]{0:T(128)S(1)} %stack.112.which_ref, bf16[16,64,256]{2,1,0:T(8,128)(2,1)S(1)} %bitcast.147, bf16[16,64,256]{2,1,0:T(8,128)(2,1)S(1)} %collective-permute-done.1.refs_1_, bf16[16,64,256]{2,1,0:T(8,128)(2,1)S(1)} %collective-permute-done.3.refs_2_, ...), custom_call_target="tpu_custom_call", output_to_operand_aliasing={{}: (12, {})} | custom-call | flops 19327352832 | bytes 26214400 | tf_op jit(solution)/shard_map/ladder/pallas_call | solution.py:95
  521.1 18.8 %ladder.11 = f32[32,64,256]{2,1,0:T(8,128)} custom-call(s32[8]{0:T(128)S(1)} %stack.101.which_ref, bf16[16,64,256]{2,1,0:T(8,128)(2,1)S(1)} %copy-done.11, bf16[16,64,256]{2,1,0:T(8,128)(2,1)S(1)} %copy-done.13, bf16[16,64,256]{2,1,0:T(8,128)(2,1)S(1)} %copy-done.15, bf16[16,64,256]{2,1,0:T(8,128)(2,1)} %copy-done.50, ...), custom_call_target="tpu_custom_call", output_to_operand_aliasing={{}: (8, {})} | custom-call | flops 10737418240 | bytes 15728640 | tf_op jit(solution)/shard_map/ladder/pallas_call | solution.py:95
  541.4 2.8 collective-permute-done.54
  547.0 2.1 collective-permute-start.57
  550.0 5.8 %collective-permute-done.57 = f32[2,4,16,512]{3,2,1,0:T(8,128)S(1)} collective-permute-done((f32[2,4,16,512]{3,2,1,0:T(8,128)S(1)}, f32[2,4,16,512]{3,2,1,0:T(8,128)S(1)}, u32[]{:S(2)}, u32[]{:S(2)}) %collective-permute-start.57) | collective-permute-done | bytes 262176 | tf_op jit(solution)/shard_map/ppermute | solution.py:133
  558.5 2.4 collective-permute-done.58
  562.5 4.0 collective-permute-start.59
  569.0 3.1 collective-permute-done.60
  (241 shorter events, 82.2 us)
Async XLA Ops:
  3.2 64.9 %collective-permute-start.15 = (bf16[2,32,64,256]{3,2,1,0:T(8,128)(2,1)}, bf16[2,32,64,256]{3,2,1,0:T(8,128)(2,1)}, u32[]{:S(2)}, u32[]{:S(2)}) collective-permute-start(bf16[2,32,64,256]{3,2,1,0:T(8,128)(2,1)} %bitcast.97.clone.2), channel_id=1, source_target_pairs={{0,4},{1,5},{2,6},{3,7},{4,0},{5,1},{6,2},{7,3},{8,12},{9,13},{10,... | collective-permute-start | bytes 6291464 | tf_op jit(solution)/shard_map/ppermute | solution.py:133
  25.0 38.2 %collective-permute-start.42 = (bf16[16,64,256]{2,1,0:T(8,128)(2,1)}, bf16[16,64,256]{2,1,0:T(8,128)(2,1)S(1)}, u32[]{:S(2)}, u32[]{:S(2)}) collective-permute-start(bf16[16,64,256]{2,1,0:T(8,128)(2,1)} %bitcast.57), channel_id=1, source_target_pairs={{0,4},{1,5},{2,6},{3,7},{4,0},{5,1},{6,2},{7,3},{8,12},{9,13},{10,... | collective-permute-start | bytes 1572872 | tf_op jit(solution)/shard_map/ppermute | solution.py:133
  26.6 38.4 %collective-permute-start.43 = (bf16[16,64,256]{2,1,0:T(8,128)(2,1)S(1)}, bf16[16,64,256]{2,1,0:T(8,128)(2,1)S(1)}, u32[]{:S(2)}, u32[]{:S(2)}) collective-permute-start(bf16[16,64,256]{2,1,0:T(8,128)(2,1)S(1)} %bitcast.142), channel_id=1, source_target_pairs={{0,8},{1,9},{2,10},{3,11},{4,12},{5,13},{6,14},{7,15},{8,0},{9,1},... | collective-permute-start | bytes 1572872 | tf_op jit(solution)/shard_map/ppermute | solution.py:133
  28.7 37.8 %collective-permute-start.45 = (bf16[16,64,256]{2,1,0:T(8,128)(2,1)S(1)}, bf16[16,64,256]{2,1,0:T(8,128)(2,1)}, u32[]{:S(2)}, u32[]{:S(2)}) collective-permute-start(bf16[16,64,256]{2,1,0:T(8,128)(2,1)S(1)} %bitcast.143), channel_id=1, source_target_pairs={{8,16},{9,17},{10,18},{11,19},{12,20},{13,21},{14,22},{15,23},{16,... | collective-permute-start | bytes 1572872 | tf_op jit(solution)/shard_map/ppermute | solution.py:133
  30.2 93.1 %collective-permute-start.7 = (bf16[2,32,64,256]{3,2,1,0:T(8,128)(2,1)}, bf16[2,32,64,256]{3,2,1,0:T(8,128)(2,1)}, u32[]{:S(2)}, u32[]{:S(2)}) collective-permute-start(bf16[2,32,64,256]{3,2,1,0:T(8,128)(2,1)} %bitcast.97.clone.2), channel_id=1, source_target_pairs={{2,10},{3,11},{6,14},{7,15},{24,16},{25,17},{28,20},{29,21}} | collective-permute-start | bytes 6291464 | tf_op jit(solution)/shard_map/ppermute | solution.py:133
  66.5 69.9 %collective-permute-start.17 = (bf16[2,32,64,256]{3,2,1,0:T(8,128)(2,1)}, bf16[2,32,64,256]{3,2,1,0:T(8,128)(2,1)S(1)}, u32[]{:S(2)}, u32[]{:S(2)}) collective-permute-start(bf16[2,32,64,256]{3,2,1,0:T(8,128)(2,1)} %bitcast.97.clone.2), channel_id=1, source_target_pairs={{0,2},{1,3},{2,0},{3,1},{4,6},{5,7},{6,4},{7,5},{8,10},{9,11},{10,... | collective-permute-start | bytes 6291464 | tf_op jit(solution)/shard_map/ppermute | solution.py:133
  68.0 89.6 %collective-permute-start.18 = (bf16[2,32,64,256]{3,2,1,0:T(8,128)(2,1)}, bf16[2,32,64,256]{3,2,1,0:T(8,128)(2,1)S(1)}, u32[]{:S(2)}, u32[]{:S(2)}) collective-permute-start(bf16[2,32,64,256]{3,2,1,0:T(8,128)(2,1)} %collective-permute-done.15), channel_id=1, source_target_pairs={{0,2},{1,3},{2,0},{3,1},{4,6},{5,7},{6,4},{7,5},{8,10},{9,11},{10,... | collective-permute-start | bytes 6291464 | tf_op jit(solution)/shard_map/ppermute | solution.py:133
  77.5 14.4 %collective-permute-start.44 = (bf16[16,64,256]{2,1,0:T(8,128)(2,1)S(1)}, bf16[16,64,256]{2,1,0:T(8,128)(2,1)}, u32[]{:S(2)}, u32[]{:S(2)}) collective-permute-start(bf16[16,64,256]{2,1,0:T(8,128)(2,1)S(1)} %collective-permute-done.42.refs_1_), channel_id=1, source_target_pairs={{0,8},{1,9},{2,10},{3,11},{4,12},{5,13},{6,14},{7,15},{8,0},{9,1},... | collective-permute-start | bytes 1572872 | tf_op jit(solution)/shard_map/ppermute | solution.py:133
  92.6 35.5 %collective-permute-start.46 = (bf16[16,64,256]{2,1,0:T(8,128)(2,1)}, bf16[16,64,256]{2,1,0:T(8,128)(2,1)S(1)}, u32[]{:S(2)}, u32[]{:S(2)}) collective-permute-start(bf16[16,64,256]{2,1,0:T(8,128)(2,1)} %collective-permute-done.45), channel_id=1, source_target_pairs={{8,0},{9,1},{10,2},{11,3},{12,4},{13,5},{14,6},{15,7},{16,24},{17,... | collective-permute-start | bytes 1572872 | tf_op jit(solution)/shard_map/ppermute | solution.py:133
  93.9 41.9 %collective-permute-start.32 = (bf16[16,64,256]{2,1,0:T(8,128)(2,1)S(1)}, bf16[16,64,256]{2,1,0:T(8,128)(2,1)S(1)}, u32[]{:S(2)}, u32[]{:S(2)}) collective-permute-start(bf16[16,64,256]{2,1,0:T(8,128)(2,1)S(1)} %collective-permute-done.30.refs_1_), channel_id=1, source_target_pairs={{0,8},{1,9},{2,10},{3,11},{4,12},{5,13},{6,14},{7,15},{8,0},{9,1},... | collective-permute-start | bytes 1572872 | tf_op jit(solution)/shard_map/ppermute | solution.py:133
  123.3 91.7 %collective-permute-start.9 = (bf16[2,32,64,256]{3,2,1,0:T(8,128)(2,1)}, bf16[2,32,64,256]{3,2,1,0:T(8,128)(2,1)}, u32[]{:S(2)}, u32[]{:S(2)}) collective-permute-start(bf16[2,32,64,256]{3,2,1,0:T(8,128)(2,1)} %collective-permute-done.7), channel_id=1, source_target_pairs={{10,14},{11,15},{14,10},{15,11},{16,20},{17,21},{20,16},{21,17}} | collective-permute-start | bytes 6291464 | tf_op jit(solution)/shard_map/ppermute | solution.py:133
  128.0 40.3 %collective-permute-start.37 = (bf16[16,64,256]{2,1,0:T(8,128)(2,1)S(1)}, bf16[16,64,256]{2,1,0:T(8,128)(2,1)S(1)}, u32[]{:S(2)}, u32[]{:S(2)}) collective-permute-start(bf16[16,64,256]{2,1,0:T(8,128)(2,1)S(1)} %collective-permute-done.31.refs_2_), channel_id=1, source_target_pairs={{8,16},{9,17},{10,18},{11,19},{12,20},{13,21},{14,22},{15,23},{16,... | collective-permute-start | bytes 1572872 | tf_op jit(solution)/shard_map/ppermute | solution.py:133
  135.8 33.9 %collective-permute-start.35 = (bf16[16,64,256]{2,1,0:T(8,128)(2,1)S(1)}, bf16[16,64,256]{2,1,0:T(8,128)(2,1)S(1)}, u32[]{:S(2)}, u32[]{:S(2)}) collective-permute-start(bf16[16,64,256]{2,1,0:T(8,128)(2,1)S(1)} %collective-permute-done.30.refs_1_), channel_id=1, source_target_pairs={{8,16},{9,17},{10,18},{11,19},{12,20},{13,21},{14,22},{15,23},{16,... | collective-permute-start | bytes 1572872 | tf_op jit(solution)/shard_map/ppermute | solution.py:133
  136.5 33.3 %collective-permute-start.34 = (bf16[16,64,256]{2,1,0:T(8,128)(2,1)S(1)}, bf16[16,64,256]{2,1,0:T(8,128)(2,1)S(1)}, u32[]{:S(2)}, u32[]{:S(2)}) collective-permute-start(bf16[16,64,256]{2,1,0:T(8,128)(2,1)S(1)} %collective-permute-done.33), channel_id=1, source_target_pairs={{8,0},{9,1},{10,2},{11,3},{12,4},{13,5},{14,6},{15,7},{16,24},{17,... | collective-permute-start | bytes 1572872 | tf_op jit(solution)/shard_map/ppermute | solution.py:133
  157.6 22.2 %collective-permute-start.51 = (bf16[16,64,256]{2,1,0:T(8,128)(2,1)}, bf16[16,64,256]{2,1,0:T(8,128)(2,1)}, u32[]{:S(2)}, u32[]{:S(2)}) collective-permute-start(bf16[16,64,256]{2,1,0:T(8,128)(2,1)} %collective-permute-done.44.refs_3_), channel_id=1, source_target_pairs={{8,16},{9,17},{10,18},{11,19},{12,20},{13,21},{14,22},{15,23},{16,... | collective-permute-start | bytes 1572872 | tf_op jit(solution)/shard_map/ppermute | solution.py:133
  168.4 17.4 %collective-permute-start.50 = (bf16[16,64,256]{2,1,0:T(8,128)(2,1)}, bf16[16,64,256]{2,1,0:T(8,128)(2,1)}, u32[]{:S(2)}, u32[]{:S(2)}) collective-permute-start(bf16[16,64,256]{2,1,0:T(8,128)(2,1)} %collective-permute-done.49), channel_id=1, source_target_pairs={{8,0},{9,1},{10,2},{11,3},{12,4},{13,5},{14,6},{15,7},{16,24},{17,... | collective-permute-start | bytes 1572872 | tf_op jit(solution)/shard_map/ppermute | solution.py:133
  169.7 93.7 %collective-permute-start.16 = (bf16[2,32,2,64,256]{4,3,1,0,2:T(8,128)(2,1)}, bf16[2,32,2,64,256]{4,3,1,0,2:T(8,128)(2,1)}, u32[]{:S(2)}, u32[]{:S(2)}) collective-permute-start(bf16[2,32,2,64,256]{4,3,1,0,2:T(8,128)(2,1)} %get-tuple-element.14), channel_id=1, source_target_pairs={{0,1},{1,0},{2,3},{3,2},{4,5},{5,4},{6,7},{7,6},{8,9},{9,8},{10,11... | collective-permute-start | bytes 12582920 | tf_op jit(solution)/shard_map/ppermute | solution.py:133
  169.8 95.1 %collective-permute-start.19 = (bf16[2,32,2,64,256]{4,3,1,0,2:T(8,128)(2,1)}, bf16[2,32,2,64,256]{4,3,1,0,2:T(8,128)(2,1)}, u32[]{:S(2)}, u32[]{:S(2)}) collective-permute-start(bf16[2,32,2,64,256]{4,3,1,0,2:T(8,128)(2,1)} %get-tuple-element.16), channel_id=1, source_target_pairs={{0,1},{1,0},{2,3},{3,2},{4,5},{5,4},{6,7},{7,6},{8,9},{9,8},{10,11... | collective-permute-start | bytes 12582920 | tf_op jit(solution)/shard_map/ppermute | solution.py:133
  179.8 18.3 %collective-permute-start.48 = (bf16[16,64,256]{2,1,0:T(8,128)(2,1)}, bf16[16,64,256]{2,1,0:T(8,128)(2,1)S(1)}, u32[]{:S(2)}, u32[]{:S(2)}) collective-permute-start(bf16[16,64,256]{2,1,0:T(8,128)(2,1)} %copy-done.26), channel_id=1, source_target_pairs={{8,0},{9,1},{10,2},{11,3},{12,4},{13,5},{14,6},{15,7},{16,24},{17,... | collective-permute-start | bytes 1572872 | tf_op jit(solution)/shard_map/ppermute | solution.py:133
  185.8 15.0 %collective-permute-start.39 = (bf16[16,64,256]{2,1,0:T(8,128)(2,1)S(1)}, bf16[16,64,256]{2,1,0:T(8,128)(2,1)S(1)}, u32[]{:S(2)}, u32[]{:S(2)}) collective-permute-start(bf16[16,64,256]{2,1,0:T(8,128)(2,1)S(1)} %copy-done.43), channel_id=1, source_target_pairs={{8,16},{9,17},{10,18},{11,19},{12,20},{13,21},{14,22},{15,23},{16,... | collective-permute-start | bytes 1572872 | tf_op jit(solution)/shard_map/ppermute | solution.py:133
  198.1 15.6 %collective-permute-start.38 = (bf16[16,64,256]{2,1,0:T(8,128)(2,1)S(1)}, bf16[16,64,256]{2,1,0:T(8,128)(2,1)S(1)}, u32[]{:S(2)}, u32[]{:S(2)}) collective-permute-start(bf16[16,64,256]{2,1,0:T(8,128)(2,1)S(1)} %copy-done.31), channel_id=1, source_target_pairs={{8,0},{9,1},{10,2},{11,3},{12,4},{13,5},{14,6},{15,7},{16,24},{17,... | collective-permute-start | bytes 1572872 | tf_op jit(solution)/shard_map/ppermute | solution.py:133
  200.8 56.4 %collective-permute-start.8 = (bf16[2,32,64,256]{3,2,1,0:T(8,128)(2,1)}, bf16[2,32,64,256]{3,2,1,0:T(8,128)(2,1)S(1)}, u32[]{:S(2)}, u32[]{:S(2)}) collective-permute-start(bf16[2,32,64,256]{3,2,1,0:T(8,128)(2,1)} %collective-permute-done.7), channel_id=1, source_target_pairs={{10,8},{11,9},{14,12},{15,13},{16,18},{17,19},{20,22},{21,23}} | collective-permute-start | bytes 6291464 | tf_op jit(solution)/shard_map/ppermute | solution.py:133
  213.7 14.7 %collective-permute-start.36 = (bf16[16,64,256]{2,1,0:T(8,128)(2,1)S(1)}, bf16[16,64,256]{2,1,0:T(8,128)(2,1)S(1)}, u32[]{:S(2)}, u32[]{:S(2)}) collective-permute-start(bf16[16,64,256]{2,1,0:T(8,128)(2,1)S(1)} %copy-done.29), channel_id=1, source_target_pairs={{8,0},{9,1},{10,2},{11,3},{12,4},{13,5},{14,6},{15,7},{16,24},{17,... | collective-permute-start | bytes 1572872 | tf_op jit(solution)/shard_map/ppermute | solution.py:133
  215.0 43.2 %collective-permute-start.10 = (bf16[2,32,64,256]{3,2,1,0:T(8,128)(2,1)}, bf16[2,32,64,256]{3,2,1,0:T(8,128)(2,1)S(1)}, u32[]{:S(2)}, u32[]{:S(2)}) collective-permute-start(bf16[2,32,64,256]{3,2,1,0:T(8,128)(2,1)} %collective-permute-done.9), channel_id=1, source_target_pairs={{10,8},{11,9},{14,12},{15,13},{16,18},{17,19},{20,22},{21,23}} | collective-permute-start | bytes 6291464 | tf_op jit(solution)/shard_map/ppermute | solution.py:133
  228.4 14.0 %collective-permute-start.52 = (bf16[16,64,256]{2,1,0:T(8,128)(2,1)}, bf16[16,64,256]{2,1,0:T(8,128)(2,1)S(1)}, u32[]{:S(2)}, u32[]{:S(2)}) collective-permute-start(bf16[16,64,256]{2,1,0:T(8,128)(2,1)} %collective-permute-done.51), channel_id=1, source_target_pairs={{8,0},{9,1},{10,2},{11,3},{12,4},{13,5},{14,6},{15,7},{16,24},{17,... | collective-permute-start | bytes 1572872 | tf_op jit(solution)/shard_map/ppermute | solution.py:133
  256.3 112.2 %collective-permute-start.23 = (bf16[16,64,256]{2,1,0:T(8,128)(2,1)S(1)}, bf16[16,64,256]{2,1,0:T(8,128)(2,1)S(1)}, u32[]{:S(2)}, u32[]{:S(2)}) collective-permute-start(bf16[16,64,256]{2,1,0:T(8,128)(2,1)S(1)} %bitcast.148), channel_id=1, source_target_pairs={{0,8},{1,9},{2,10},{3,11},{4,12},{5,13},{6,14},{7,15},{8,0},{9,1},... | collective-permute-start | bytes 1572872 | tf_op jit(solution)/shard_map/ppermute | solution.py:133
  257.2 111.9 %collective-permute-start.20 = (bf16[16,64,256]{2,1,0:T(8,128)(2,1)S(1)}, bf16[16,64,256]{2,1,0:T(8,128)(2,1)S(1)}, u32[]{:S(2)}, u32[]{:S(2)}) collective-permute-start(bf16[16,64,256]{2,1,0:T(8,128)(2,1)S(1)} %bitcast.149), channel_id=1, source_target_pairs={{8,16},{9,17},{10,18},{11,19},{12,20},{13,21},{14,22},{15,23},{16,... | collective-permute-start | bytes 1572872 | tf_op jit(solution)/shard_map/ppermute | solution.py:133
  258.1 20.5 %collective-permute-start.53 = (bf16[16,64,256]{2,1,0:T(8,128)(2,1)S(1)}, bf16[16,64,256]{2,1,0:T(8,128)(2,1)S(1)}, u32[]{:S(2)}, u32[]{:S(2)}) collective-permute-start(bf16[16,64,256]{2,1,0:T(8,128)(2,1)S(1)} %get-tuple-element.21), channel_id=1, source_target_pairs={{0,4},{1,5},{2,6},{3,7},{4,0},{5,1},{6,2},{7,3},{8,12},{9,13},{10,... | collective-permute-start | bytes 1572872 | tf_op jit(solution)/shard_map/ppermute | solution.py:133
  263.4 74.3 %collective-permute-start.41 = (bf16[16,64,256]{2,1,0:T(8,128)(2,1)S(1)}, bf16[16,64,256]{2,1,0:T(8,128)(2,1)S(1)}, u32[]{:S(2)}, u32[]{:S(2)}) collective-permute-start(bf16[16,64,256]{2,1,0:T(8,128)(2,1)S(1)} %get-tuple-element.22), channel_id=1, source_target_pairs={{0,4},{1,5},{2,6},{3,7},{4,0},{5,1},{6,2},{7,3},{8,12},{9,13},{10,... | collective-permute-start | bytes 1572872 | tf_op jit(solution)/shard_map/ppermute | solution.py:133
  264.9 30.3 %collective-permute-start.21 = (bf16[16,64,256]{2,1,0:T(8,128)(2,1)S(1)}, bf16[16,64,256]{2,1,0:T(8,128)(2,1)S(1)}, u32[]{:S(2)}, u32[]{:S(2)}) collective-permute-start(bf16[16,64,256]{2,1,0:T(8,128)(2,1)S(1)} %bitcast.160), channel_id=1, source_target_pairs={{0,4},{1,5},{2,6},{3,7},{4,0},{5,1},{6,2},{7,3},{8,12},{9,13},{10,... | collective-permute-start | bytes 1572872 | tf_op jit(solution)/shard_map/ppermute | solution.py:133
  279.4 90.4 %collective-permute-start.28 = (bf16[16,64,256]{2,1,0:T(8,128)(2,1)}, bf16[16,64,256]{2,1,0:T(8,128)(2,1)S(1)}, u32[]{:S(2)}, u32[]{:S(2)}) collective-permute-start(bf16[16,64,256]{2,1,0:T(8,128)(2,1)} %get-tuple-element.23), channel_id=1, source_target_pairs={{0,4},{1,5},{2,6},{3,7},{4,0},{5,1},{6,2},{7,3},{8,12},{9,13},{10,... | collective-permute-start | bytes 1572872 | tf_op jit(solution)/shard_map/ppermute | solution.py:133
  295.2 75.3 %collective-permute-start.25 = (bf16[16,64,256]{2,1,0:T(8,128)(2,1)S(1)}, bf16[16,64,256]{2,1,0:T(8,128)(2,1)S(1)}, u32[]{:S(2)}, u32[]{:S(2)}) collective-permute-start(bf16[16,64,256]{2,1,0:T(8,128)(2,1)S(1)} %collective-permute-done.21.refs_1_), channel_id=1, source_target_pairs={{0,8},{1,9},{2,10},{3,11},{4,12},{5,13},{6,14},{7,15},{8,0},{9,1},... | collective-permute-start | bytes 1572872 | tf_op jit(solution)/shard_map/ppermute | solution.py:133
  338.5 102.1 %collective-permute-start.11 = (bf16[2,32,2,64,256]{4,3,2,1,0:T(8,128)(2,1)}, bf16[2,32,2,64,256]{4,3,2,1,0:T(8,128)(2,1)S(1)}, u32[]{:S(2)}, u32[]{:S(2)}) collective-permute-start(bf16[2,32,2,64,256]{4,3,2,1,0:T(8,128)(2,1)} %get-tuple-element.20), channel_id=1, source_target_pairs={{0,1},{1,0},{2,3},{3,2},{4,5},{5,4},{6,7},{7,6},{8,9},{9,8},{10,11... | collective-permute-start | bytes 12582920 | tf_op jit(solution)/shard_map/ppermute | solution.py:133
  368.5 31.9 %collective-permute-start.1 = (bf16[16,64,256]{2,1,0:T(8,128)(2,1)S(1)}, bf16[16,64,256]{2,1,0:T(8,128)(2,1)S(1)}, u32[]{:S(2)}, u32[]{:S(2)}) collective-permute-start(bf16[16,64,256]{2,1,0:T(8,128)(2,1)S(1)} %bitcast.159), channel_id=1, source_target_pairs={{0,4},{1,5},{2,6},{3,7},{4,0},{5,1},{6,2},{7,3},{8,12},{9,13},{10,... | collective-permute-start | bytes 1572872 | tf_op jit(solution)/shard_map/ppermute | solution.py:133
  369.1 38.2 %collective-permute-start.22 = (bf16[16,64,256]{2,1,0:T(8,128)(2,1)S(1)}, bf16[16,64,256]{2,1,0:T(8,128)(2,1)S(1)}, u32[]{:S(2)}, u32[]{:S(2)}) collective-permute-start(bf16[16,64,256]{2,1,0:T(8,128)(2,1)S(1)} %collective-permute-done.21.refs_1_), channel_id=1, source_target_pairs={{8,16},{9,17},{10,18},{11,19},{12,20},{13,21},{14,22},{15,23},{16,... | collective-permute-start | bytes 1572872 | tf_op jit(solution)/shard_map/ppermute | solution.py:133
  369.8 37.6 %collective-permute-start.24 = (bf16[16,64,256]{2,1,0:T(8,128)(2,1)S(1)}, bf16[16,64,256]{2,1,0:T(8,128)(2,1)S(1)}, u32[]{:S(2)}, u32[]{:S(2)}) collective-permute-start(bf16[16,64,256]{2,1,0:T(8,128)(2,1)S(1)} %collective-permute-done.23.refs_2_), channel_id=1, source_target_pairs={{8,16},{9,17},{10,18},{11,19},{12,20},{13,21},{14,22},{15,23},{16,... | collective-permute-start | bytes 1572872 | tf_op jit(solution)/shard_map/ppermute | solution.py:133
  370.6 41.6 %collective-permute-start.26 = (bf16[16,64,256]{2,1,0:T(8,128)(2,1)S(1)}, bf16[16,64,256]{2,1,0:T(8,128)(2,1)}, u32[]{:S(2)}, u32[]{:S(2)}) collective-permute-start(bf16[16,64,256]{2,1,0:T(8,128)(2,1)S(1)} %collective-permute-done.25.refs_3_), channel_id=1, source_target_pairs={{8,16},{9,17},{10,18},{11,19},{12,20},{13,21},{14,22},{15,23},{16,... | collective-permute-start | bytes 1572872 | tf_op jit(solution)/shard_map/ppermute | solution.py:133
  400.5 49.8 %collective-permute-start.27 = (bf16[16,64,256]{2,1,0:T(8,128)(2,1)S(1)}, bf16[16,64,256]{2,1,0:T(8,128)(2,1)S(1)}, u32[]{:S(2)}, u32[]{:S(2)}) collective-permute-start(bf16[16,64,256]{2,1,0:T(8,128)(2,1)S(1)} %copy-done.38), channel_id=1, source_target_pairs={{0,8},{1,9},{2,10},{3,11},{4,12},{5,13},{6,14},{7,15},{24,16},{25,... | collective-permute-start | bytes 1572872 | tf_op jit(solution)/shard_map/ppermute | solution.py:133
  407.4 44.5 %collective-permute-start.3 = (bf16[16,64,256]{2,1,0:T(8,128)(2,1)S(1)}, bf16[16,64,256]{2,1,0:T(8,128)(2,1)S(1)}, u32[]{:S(2)}, u32[]{:S(2)}) collective-permute-start(bf16[16,64,256]{2,1,0:T(8,128)(2,1)S(1)} %bitcast.145), channel_id=1, source_target_pairs={{0,8},{1,9},{2,10},{3,11},{4,12},{5,13},{6,14},{7,15},{8,0},{9,1},... | collective-permute-start | bytes 1572872 | tf_op jit(solution)/shard_map/ppermute | solution.py:133
  407.5 45.1 %collective-permute-start.29 = (bf16[16,64,256]{2,1,0:T(8,128)(2,1)S(1)}, bf16[16,64,256]{2,1,0:T(8,128)(2,1)}, u32[]{:S(2)}, u32[]{:S(2)}) collective-permute-start(bf16[16,64,256]{2,1,0:T(8,128)(2,1)S(1)} %collective-permute-done.28.refs_10_), channel_id=1, source_target_pairs={{0,8},{1,9},{2,10},{3,11},{4,12},{5,13},{6,14},{7,15},{24,16},{25,... | collective-permute-start | bytes 1572872 | tf_op jit(solution)/shard_map/ppermute | solution.py:133
  412.2 41.1 %collective-permute-start.5 = (bf16[16,64,256]{2,1,0:T(8,128)(2,1)S(1)}, bf16[16,64,256]{2,1,0:T(8,128)(2,1)}, u32[]{:S(2)}, u32[]{:S(2)}) collective-permute-start(bf16[16,64,256]{2,1,0:T(8,128)(2,1)S(1)} %collective-permute-done.1.refs_1_), channel_id=1, source_target_pairs={{0,8},{1,9},{2,10},{3,11},{4,12},{5,13},{6,14},{7,15},{8,0},{9,1},... | collective-permute-start | bytes 1572872 | tf_op jit(solution)/shard_map/ppermute | solution.py:133
  440.6 32.5 %collective-permute-start = (bf16[16,64,256]{2,1,0:T(8,128)(2,1)S(1)}, bf16[16,64,256]{2,1,0:T(8,128)(2,1)S(1)}, u32[]{:S(2)}, u32[]{:S(2)}) collective-permute-start(bf16[16,64,256]{2,1,0:T(8,128)(2,1)S(1)} %bitcast.146), channel_id=1, source_target_pairs={{8,16},{9,17},{10,18},{11,19},{12,20},{13,21},{14,22},{15,23},{16,... | collective-permute-start | bytes 1572872 | tf_op jit(solution)/shard_map/ppermute | solution.py:133
  450.3 34.4 %collective-permute-start.13 = (bf16[16,64,256]{2,1,0:T(8,128)(2,1)S(1)}, bf16[16,64,256]{2,1,0:T(8,128)(2,1)S(1)}, u32[]{:S(2)}, u32[]{:S(2)}) collective-permute-start(bf16[16,64,256]{2,1,0:T(8,128)(2,1)S(1)} %copy-done.37), channel_id=1, source_target_pairs={{0,4},{1,5},{2,6},{3,7},{4,0},{5,1},{6,2},{7,3},{8,12},{9,13},{10,... | collective-permute-start | bytes 1572872 | tf_op jit(solution)/shard_map/ppermute | solution.py:133
  451.9 34.2 %collective-permute-start.2 = (bf16[16,64,256]{2,1,0:T(8,128)(2,1)S(1)}, bf16[16,64,256]{2,1,0:T(8,128)(2,1)S(1)}, u32[]{:S(2)}, u32[]{:S(2)}) collective-permute-start(bf16[16,64,256]{2,1,0:T(8,128)(2,1)S(1)} %collective-permute-done.1.refs_1_), channel_id=1, source_target_pairs={{8,16},{9,17},{10,18},{11,19},{12,20},{13,21},{14,22},{15,23},{16,... | collective-permute-start | bytes 1572872 | tf_op jit(solution)/shard_map/ppermute | solution.py:133
  452.6 33.5 %collective-permute-start.4 = (bf16[16,64,256]{2,1,0:T(8,128)(2,1)S(1)}, bf16[16,64,256]{2,1,0:T(8,128)(2,1)S(1)}, u32[]{:S(2)}, u32[]{:S(2)}) collective-permute-start(bf16[16,64,256]{2,1,0:T(8,128)(2,1)S(1)} %collective-permute-done.3.refs_2_), channel_id=1, source_target_pairs={{8,16},{9,17},{10,18},{11,19},{12,20},{13,21},{14,22},{15,23},{16,... | collective-permute-start | bytes 1572872 | tf_op jit(solution)/shard_map/ppermute | solution.py:133
  453.3 32.8 %collective-permute-start.6 = (bf16[16,64,256]{2,1,0:T(8,128)(2,1)}, bf16[16,64,256]{2,1,0:T(8,128)(2,1)S(1)}, u32[]{:S(2)}, u32[]{:S(2)}) collective-permute-start(bf16[16,64,256]{2,1,0:T(8,128)(2,1)} %collective-permute-done.5.refs_3_), channel_id=1, source_target_pairs={{8,16},{9,17},{10,18},{11,19},{12,20},{13,21},{14,22},{15,23},{16,... | collective-permute-start | bytes 1572872 | tf_op jit(solution)/shard_map/ppermute | solution.py:133
  473.1 43.2 %collective-permute-start.12 = (bf16[16,64,256]{2,1,0:T(8,128)(2,1)S(1)}, bf16[16,64,256]{2,1,0:T(8,128)(2,1)S(1)}, u32[]{:S(2)}, u32[]{:S(2)}) collective-permute-start(bf16[16,64,256]{2,1,0:T(8,128)(2,1)S(1)} %copy-done.36), channel_id=1, source_target_pairs={{0,8},{1,9},{2,10},{3,11},{4,12},{5,13},{6,14},{7,15},{24,16},{25,... | collective-permute-start | bytes 1572872 | tf_op jit(solution)/shard_map/ppermute | solution.py:133
  484.8 31.6 %collective-permute-start.14 = (bf16[16,64,256]{2,1,0:T(8,128)(2,1)S(1)}, bf16[16,64,256]{2,1,0:T(8,128)(2,1)S(1)}, u32[]{:S(2)}, u32[]{:S(2)}) collective-permute-start(bf16[16,64,256]{2,1,0:T(8,128)(2,1)S(1)} %collective-permute-done.13.refs_10_), channel_id=1, source_target_pairs={{0,8},{1,9},{2,10},{3,11},{4,12},{5,13},{6,14},{7,15},{24,16},{25,... | collective-permute-start | bytes 1572872 | tf_op jit(solution)/shard_map/ppermute | solution.py:133
  (67 other events, 1091.2 us)

commit v2 on v1

v2 whole, which is shorter than its diff:
```python
import functools

import jax
import jax.numpy as jnp
from jax import lax
from jax.experimental import pallas as pl
from jax.experimental.pallas import tpu as pltpu
from jax.sharding import PartitionSpec as P

AXES = ("row", "col")
IN_FLIGHT = 5


def contract_aux(left_piece, right_piece):
    return lax.dot_general(
        left_piece, right_piece, (((2,), (1,)), ((), ())), preferred_element_type=jnp.float32
    )


def gathered_whole(left_factors, right_factors, amplitudes, eps_left, eps_right, pair_energy):
    width_a, local_c, _ = left_factors.shape
    local_d = right_factors.shape[0]
    width_b = eps_right.shape[0]
    pairs = amplitudes.shape[2]
    gathered = lax.all_gather(right_factors, "row", axis=1, tiled=True)
    right_whole = gathered.reshape(local_d, -1, width_b)
    left_whole = lax.all_gather(left_factors, "col", axis=2, tiled=True)
    integ = contract_aux(left_whole, right_whole)
    integ = integ.astype(jnp.bfloat16)
    n_row = lax.axis_size("row")
    n_col = lax.axis_size("col")
    own_pairs = pairs // n_row
    own_a = width_a // n_col
    partial_value = jnp.einsum(
        "cdp,acdb->pab", amplitudes, integ, preferred_element_type=jnp.float32
    )
    partial_value = partial_value.reshape(pairs, width_a * width_b)
    section = lax.psum_scatter(partial_value, "row", scatter_dimension=0, tiled=True)
    ladder = lax.psum_scatter(section, "col", scatter_dimension=1, tiled=True)
    ladder = ladder.reshape(own_pairs, own_a, width_b)
    denom = eps_left[None, :, None] + eps_right[None, None, :] - pair_energy[:, None, None]
    return ladder / denom


def ladder_kernel(slots, n_left, first, which_ref, *refs):
    pieces, refs = refs[:slots], refs[slots:]
    lefts, refs = refs[: 4 * n_left], refs[4 * n_left :]
    amp_own_ref, amp_other_ref, *add_ref, out_ref, held, sems = refs
    depth, width_b, width_q = pieces[0].shape
    _, _, _, tile_a, _, chunk_c, _ = held.shape
    span = 2 * chunk_c
    step, steps = pl.program_id(0), pl.num_programs(0)

    def copies(at, slot):
        rows = pl.ds(pl.multiple_of(at * tile_a, tile_a), tile_a)
        return [
            pltpu.make_async_copy(
                lefts[4 * r + 2 * s + h].at[rows], held.at[slot, r, h, :, s], sems.at[slot, r, s, h]
            )
            for r in range(n_left)
            for s in range(2)
            for h in range(2)
        ]

    @pl.when(step == 0)
    def _():
        for copy in copies(step, 0):
            copy.start()

    slot = lax.rem(step, 2)

    @pl.when(step + 1 < steps)
    def _():
        for copy in copies(step + 1, 1 - slot):
            copy.start()

    for copy in copies(step, slot):
        copy.wait()

    integ = None
    for s in range(slots):
        left = held[slot, which_ref[2 * s], which_ref[2 * s + 1]].reshape(tile_a * span, width_q)
        right = pieces[s][...].reshape(depth * width_b, width_q)
        term = lax.dot_general(
            right, left, (((1,), (1,)), ((), ())), preferred_element_type=jnp.float32
        )
        integ = term if integ is None else integ + term
    integ = integ.astype(jnp.bfloat16)
    integ = jnp.concatenate(
        [
            jnp.concatenate(
                [
                    integ[d * width_b : (d + 1) * width_b, a * span : (a + 1) * span]
                    for d in range(depth)
                ],
                axis=1,
            )
            for a in range(tile_a)
        ],
        axis=0,
    )
    amp = jnp.concatenate([amp_own_ref[...], amp_other_ref[...]], axis=1)
    amp = amp.reshape(depth * span, -1)
    out = jnp.dot(integ, amp, preferred_element_type=jnp.float32).reshape(out_ref.shape)
    out_ref[...] = out if first else add_ref[0][...] + out


def add_ladder(pieces, which, lefts, amps, add, depth, tile_a=4):
    slots, n_left = len(pieces), len(lefts) // 4
    width_b, width_q = pieces[0][0].shape[-2:]
    width_a, chunk_c = lefts[0].shape[:2]
    pairs = amps[0][0].shape[-1]

    def chunk_of(array, at):
        if array.ndim == 4:
            return pl.BlockSpec((None, *array.shape[1:]), lambda i, w: (at, 0, 0, 0))
        return pl.BlockSpec((depth, *array.shape[1:]), lambda i, w: (at, 0, 0))

    out_spec = pl.BlockSpec((tile_a, width_b, pairs), lambda i, w: (i, 0, 0))
    products = depth * width_b * width_a * 2 * chunk_c * (slots * width_q + pairs)
    moved = 2 * depth * (slots * width_b * width_q + 2 * chunk_c * pairs)
    moved += sum(2 * v.size for v in lefts) + 8 * width_a * width_b * pairs
    more = () if add is None else (add,)
    return pl.pallas_call(
        functools.partial(ladder_kernel, slots, n_left, add is None),
        grid_spec=pltpu.PrefetchScalarGridSpec(
            num_scalar_prefetch=1,
            grid=(width_a // tile_a,),
            in_specs=[chunk_of(*v) for v in pieces]
            + [pl.BlockSpec(memory_space=pl.ANY)] * len(lefts)
            + [chunk_of(*v) for v in amps]
            + [out_spec] * len(more),
            out_specs=out_spec,
            scratch_shapes=[
                pltpu.VMEM((2, n_left, 2, tile_a, 2, chunk_c, width_q), jnp.bfloat16),
                pltpu.SemaphoreType.DMA((2, n_left, 2, 2)),
            ],
        ),
        out_shape=jax.ShapeDtypeStruct((width_a, width_b, pairs), jnp.float32),
        input_output_aliases={slots + len(lefts) + 3: 0} if more else {},
        cost_estimate=pl.CostEstimate(flops=2 * products, bytes_accessed=moved, transcendentals=0),
        compiler_params=pltpu.CompilerParams(vmem_limit_bytes=32 * 2**20),
        name="ladder",
    )(which, *(v for v, _ in pieces), *lefts, *(v for v, _ in amps), *more)


def by_lines(n_row, n_col, *arrays):
    left_factors, right_factors, amplitudes, eps_left, eps_right, pair_energy = arrays
    row, col = lax.axis_index("row"), lax.axis_index("col")
    n_z, n_y = n_row // 2, n_col // 2
    z, x, y, core = row // 2, row % 2, col // 2, col % 2
    half = n_z // 2

    def inner(at):
        return at in (half - 1, half)

    issued = []
    latest = []

    def send(value, place):
        pairs = []
        for at_z in range(n_z):
            for at_x in range(2):
                for at_y in range(n_y):
                    for at_k in range(2):
                        to = place(at_z, at_x, at_y, at_k)
                        if to is not None:
                            source = (at_z * 2 + at_x) * n_col + at_y * 2 + at_k
                            target = (to[0] * 2 + to[1]) * n_col + to[2] * 2 + to[3]
                            pairs.append((source, target))
        value, *_ = lax.optimization_barrier((value, *issued[-IN_FLIGHT:][:1], *latest))
        got = lax.ppermute(value, AXES, pairs)
        issued.append(got)
        return got

    def other_x(c, x, y, k):
        return c, 1 - x, y, k

    def other_y(c, x, y, k):
        return c, x, 1 - y, k

    def other_core(c, x, y, k):
        return c, x, y, 1 - k

    def near(c, x, y, k):
        return c ^ 1, x, y, k

    def across(c, x, y, k):
        return (n_z - 1 - c, x, y, k) if inner(c) else None

    def outward(c, x, y, k):
        return (c ^ 1, x, y, k) if inner(c) else None

    def between_inner(step):
        return lambda c, x, y, k: step(c, x, y, k) if inner(c) else None

    is_inner = (z == half - 1) | (z == half)
    at_far = y == 1 - z // half

    width_a, local_c, local_q = left_factors.shape
    mine = left_factors.reshape(width_a, local_c, 2, local_q // 2).transpose(2, 0, 1, 3)

    local_d = right_factors.shape[0]
    width_b = eps_right.shape[0]
    part_d = local_d // 4
    depth = part_d // 2

    def right_part(at_x, part):
        rows = lax.dynamic_slice_in_dim(right_factors, at_x * 2 * part_d + part * part_d, part_d)
        return rows.reshape(part_d, -1, width_b).transpose(0, 2, 1)

    def amp_part(at_x, part):
        got = lax.dynamic_slice_in_dim(amplitudes, at_x * 2 * part_d + part * part_d, part_d, 1)
        return got.transpose(1, 0, 2)

    def both(one, two, at):
        rows = slice(at * depth, (at + 1) * depth)
        return jnp.stack([one[rows], two[rows]])

    def swap(inner_one, end_one):
        return send(jnp.where(is_inner, inner_one, end_one.reshape(inner_one.shape)), near)

    far_inner = jnp.where(z < half, half, half - 1)
    planes = (z, z ^ 1, far_inner, far_inner ^ 1)
    which = jnp.stack([v for p in planes for v in (p ^ col, x, p ^ col, 1 - x)])
    turn = at_far.astype(x.dtype)
    which_end = jnp.stack(
        [v for p in planes[2:] for v in ((p % 2) ^ core, x ^ turn, (p % 2) ^ core, 1 - x ^ turn)]
    )

    y_0 = send(mine[0], other_y)
    x_full = send(right_part(1 - x, 0), other_x)
    o_full = right_part(x, 0)
    near_o = send(o_full, near)
    far_o = send(o_full, across)
    mine_k = send(mine, other_core)
    y_1 = send(mine[1], other_y)
    x_0 = send(mine[0], other_x)
    near_x = send(x_full, near)
    far_x = send(x_full, across)
    yk_0 = send(y_0, other_core)
    x_1 = send(mine[1], other_x)
    xy_0 = send(x_0, other_y)
    third_o = send(near_o, across)
    far_full = [both(far_o, far_x, i) for i in range(2)]
    e3 = swap(far_full[0], jnp.where(at_far, mine[1], y_0))
    yk_1 = send(y_1, other_core)
    x_split = send(right_part(1 - x, 1), other_x)
    xy_1 = send(x_1, other_y)
    e4 = send(far_full[1], outward)
    third_x = send(near_x, across)
    xk_0 = send(x_0, other_core)
    amp_full = (amp_part(x, 0), send(amp_part(1 - x, 0), other_x))
    xk_1 = send(x_1, other_core)
    o_split = right_part(x, 1)
    split = [both(o_split, x_split, i) for i in range(2)]
    third_full = [both(third_o, third_x, i) for i in range(2)]
    far_split, third_split = [None, None], [None, None]
    e5 = swap(third_full[0], split[0])
    far_split[0] = send(split[0], across)
    xyk_0 = send(xy_0, other_core)
    xyk_1 = send(xy_1, other_core)
    e6 = swap(third_full[1], split[1])
    amp_split = (amp_part(x, 1), send(amp_part(1 - x, 1), other_x))
    third_split[0] = send(e5, across)
    lefts = (mine[0], mine[1], x_0, x_1, mine_k[0], mine_k[1], xk_0, xk_1)
    lefts += (y_0, y_1, xy_0, xy_1, yk_0, yk_1, xyk_0, xyk_1)

    def full(i, out_far, out_third, total):
        far = jnp.where(is_inner, far_full[i], out_far)
        third = jnp.where(is_inner, third_full[i], out_third)
        pieces = [(o_full, i), (x_full, i), (near_o, i), (near_x, i)]
        pieces += [(far, 0), (far, 1), (third, 0), (third, 1)]
        return add_ladder(pieces, which, lefts, [(v, i) for v in amp_full], total, depth)

    def parted(i, e_in, e_out, total):
        beside = jnp.where(is_inner, e_in, e_out)
        pieces = [(v, h) for v in (split[i], beside, far_split[i], third_split[i]) for h in range(2)]
        return add_ladder(pieces, which, lefts, [(v, i) for v in amp_split], total, depth)

    def ended(i, amp_end, total):
        pieces = [(v, h) for v in (far_split[i], third_split[i]) for h in range(2)]
        return add_ladder(pieces, which_end, ends, [(amp_end, 0), (amp_end, 1)], total, depth)

    total = full(0, e3, e5, None)
    latest[:] = [total]
    far_split[1] = send(split[1], across)
    amp_both = [both(*amp_split, i) for i in range(2)]
    e7 = swap(split[0], amp_both[0])
    end_own = e3.reshape(y_0.shape)
    end_y = send(end_own, between_inner(other_y))
    end_x = send(end_own, between_inner(other_x))
    total = full(1, e4, e6, total)
    latest[:] = [total]
    third_split[1] = send(e6, across)
    e8 = swap(split[1], amp_both[1])
    end_xy = send(end_x, between_inner(other_y))
    ends = (end_own, end_y, end_x, end_xy)
    total = parted(0, e5, e7, total)
    latest[:] = [total]
    ends += tuple(send(v, other_core) for v in ends)
    total = parted(1, e6, e8, total)
    total = ended(0, e7, total)
    total = ended(1, e8, total)
    latest[:] = []
    issued[:] = []

    def pick(value, at):
        return lax.dynamic_index_in_dim(value, at, 0, keepdims=False)

    pairs = amplitudes.shape[2]
    own_a, own_pairs = width_a // n_col, pairs // n_row
    total = total.reshape(n_y, 2, own_a, width_b, pairs)
    keep = lax.dynamic_index_in_dim(total, core, 1, keepdims=False)
    give = lax.dynamic_index_in_dim(total, 1 - core, 1, keepdims=False)
    part = keep + send(give, other_core)
    part = part.reshape(n_y, own_a * width_b, n_z, 2, own_pairs).transpose(3, 0, 2, 4, 1)

    def over_x(v):
        return pick(v, x) + send(pick(v, 1 - x), other_x)

    def over_y(v):
        return pick(v, y) + send(pick(v, 1 - y), other_y)

    cut = own_pairs // 2
    first = over_y(over_x(part[:, :, :, :cut]))
    second = over_x(over_y(part[:, :, :, cut:].transpose(1, 0, 2, 3, 4)))
    part = jnp.concatenate([first, second], axis=1)
    ladder = pick(part, z)
    for step in range(1, n_z):
        ladder = ladder + send(pick(part, z ^ step), lambda c, x, y, k, s=step: (c ^ s, x, y, k))
    ladder = ladder.reshape(own_pairs, own_a, width_b)
    denom = eps_left[None, :, None] + eps_right[None, None, :] - pair_energy[:, None, None]
    return ladder / denom


def solution(mesh):
    n_row, n_col = mesh.shape["row"], mesh.shape["col"]
    lines = n_row == 2 * n_col and n_col == 4
    per_device = functools.partial(by_lines, n_row, n_col) if lines else gathered_whole
    in_specs = (
        P(None, "row", "col"),
        P("col", "row"),
        P("row", "col", None),
        P("col"),
        P(),
        P("row"),
    )
    out_specs = P("row", "col", None)
    return jax.shard_map(
        per_device, mesh=mesh, in_specs=in_specs, out_specs=out_specs, check_vma=False
    )
```

time: 576 us -> 426 us (0.74)
  starting transfers between devices: 160 us -> 85.7 us
  waiting for transfers between devices: 160 us -> 100 us
  other arithmetic: 38.6 us -> 12.5 us
  Pallas kernels: 151 us -> 162 us
    ppermute x62 -> x48, starting transfers between devices: 160 us -> 85.7 us  [send(): got = lax.ppermute(value, AXES, pairs)]
    ppermute x62 -> x48, waiting for transfers between devices: 160 us -> 100 us  [send(): got = lax.ppermute(value, AXES, pairs)]
    another operation x7 -> x1, other arithmetic: 28.3 us -> 1.45 us  [both(): return jnp.stack([one[rows], two[rows]])]
    reshape x1 -> x8, local copies, waits for them, and re-layouts: 11.3 us -> 24.6 us  [right_part(): return rows.reshape(part_d, -1, width_b).transpose(0, 2, 1)]
    pallas_call x6, Pallas kernels: 151 us -> 162 us  [add_ladder(): pl.pallas_call(functools.partial(ladder_kernel, slots, n_left, add is Non...]
    unnamed x114 -> x102, local copies, waits for them, and re-layouts: 21.8 us -> 15.3 us
    slice x1 -> x0, local copies, waits for them, and re-layouts: 6.42 us -> none  [by_lines(): give = [right_give[i].transpose(0, 2, 1) for i in chunks]]
  transfers between devices with their start and end apart: 62 -> 48, of which waited for: 20 -> 18; matrix products, arithmetic and copies ran while one was open for 15% -> 14% of each run, Pallas kernels for 23% -> 29%
where the time goes in v2:
time: 426 us; the launch traced here: 425 us
  Pallas kernels  162 us (38%)
  waiting for transfers between devices  100 us (23%)
  starting transfers between devices  85.7 us (20%)
  local copies, waits for them, and re-layouts  63.7 us (15%)
  other arithmetic  12.5 us (3%)
    pallas_call x6, Pallas kernels, add_ladder(): pl.pallas_call(functools.partial(ladder_kernel, slots, n_left, add is Non...  162 us
    ppermute x48, waiting for transfers between devices, send(): got = lax.ppermute(value, AXES, pairs)  100 us
    ppermute x48, starting transfers between devices, send(): got = lax.ppermute(value, AXES, pairs)  85.7 us
    reshape x8, local copies, waits for them, and re-layouts, right_part(): return rows.reshape(part_d, -1, width_b).transpose(0, 2, 1)  24.6 us
    unnamed x102, local copies, waits for them, and re-layouts  15.3 us
    another operation x8, local copies, waits for them, and re-layouts, both(): return jnp.stack([one[rows], two[rows]])  10.8 us
  transfers between devices with their start and end apart: 48, of which 18 were waited for; matrix products, arithmetic and copies ran while one was open for 14% of the time, Pallas kernels for 29%

profile of v2, /device:TPU:0, one launch (start us, length us, event | category | flops | bytes accessed | tf_op | source)
XLA Modules:
  0.0 424.5 jit_solution(17559127373722561942)
XLA Ops:
  0.0 1.9 copy.53
  1.9 1.7 slice_bitcast_fusion.2
  3.8 3.0 collective-permute-start
  6.8 3.9 constant_dynamic-slice_fusion.6
  10.6 3.2 reshape.71
  13.9 1.9 copy.33
  15.8 3.3 reshape.70
  19.0 2.7 copy.32
  21.8 8.4 %collective-permute-done.refs_16_ = bf16[32,64,256]{2,1,0:T(8,128)(2,1)S(1)} collective-permute-done((bf16[32,64,256]{2,1,0:T(8,128)(2,1)}, bf16[32,64,256]{2,1,0:T(8,128)(2,1)S(1)}, u32[]{:S(2)}, u32[]{:S(2)}) %collective-permute-start) | collective-permute-done | bytes 1048608 | tf_op jit(solution)/shard_map/ppermute | solution.py:172
  30.9 1.8 collective-permute-start.4
  32.7 4.3 %collective-permute-start.12 = (bf16[32,64,256]{2,1,0:T(8,128)(2,1)S(1)}, bf16[32,64,256]{2,1,0:T(8,128)(2,1)}, u32[]{:S(2)}, u32[]{:S(2)}) collective-permute-start(bf16[32,64,256]{2,1,0:T(8,128)(2,1)S(1)} %bitcast.124), channel_id=1, source_target_pairs={{0,8},{1,9},{2,10},{3,11},{4,12},{5,13},{6,14},{7,15},{8,0},{9,1},... | collective-permute-start | bytes 3145736 | tf_op jit(solution)/shard_map/ppermute | solution.py:172
  39.5 16.1 %collective-permute-done.4.refs_1_ = bf16[32,64,256]{2,1,0:T(8,128)(2,1)} collective-permute-done((bf16[32,64,256]{2,1,0:T(8,128)(2,1)}, bf16[32,64,256]{2,1,0:T(8,128)(2,1)}, u32[]{:S(2)}, u32[]{:S(2)}) %collective-permute-start.4) | collective-permute-done | bytes 1048608 | tf_op jit(solution)/shard_map/ppermute | solution.py:172
  58.8 5.2 %collective-permute-start.13 = (bf16[32,64,256]{2,1,0:T(8,128)(2,1)}, bf16[32,64,256]{2,1,0:T(8,128)(2,1)S(1)}, u32[]{:S(2)}, u32[]{:S(2)}) collective-permute-start(bf16[32,64,256]{2,1,0:T(8,128)(2,1)} %collective-permute-done.4.refs_1_), channel_id=1, source_target_pairs={{0,8},{1,9},{2,10},{3,11},{4,12},{5,13},{6,14},{7,15},{8,0},{9,1},... | collective-permute-start | bytes 3145736 | tf_op jit(solution)/shard_map/ppermute | solution.py:172
  66.4 2.3 slice_bitcast_fusion.10
  69.8 18.0 %collective-permute-start.16 = (bf16[2,16,64,256]{3,2,1,0:T(8,128)(2,1)}, bf16[2,16,64,256]{3,2,1,0:T(8,128)(2,1)S(1)}, u32[]{:S(2)}, u32[]{:S(2)}) collective-permute-start(bf16[2,16,64,256]{3,2,1,0:T(8,128)(2,1)} %broadcast_select_fusion.9), channel_id=1, source_target_pairs={{0,8},{1,9},{2,10},{3,11},{4,12},{5,13},{6,14},{7,15},{8,0},{9,1},... | collective-permute-start | bytes 3145736 | tf_op jit(solution)/shard_map/ppermute | solution.py:172
  88.2 1.7 collective-permute-start.17
  91.4 4.1 reshape.68
  95.5 2.7 copy.30
  98.7 11.7 %collective-permute-done.16 = bf16[2,16,64,256]{3,2,1,0:T(8,128)(2,1)S(1)} collective-permute-done((bf16[2,16,64,256]{3,2,1,0:T(8,128)(2,1)}, bf16[2,16,64,256]{3,2,1,0:T(8,128)(2,1)S(1)}, u32[]{:S(2)}, u32[]{:S(2)}) %collective-permute-start.16) | collective-permute-done | bytes 1048608 | tf_op jit(solution)/shard_map/ppermute | solution.py:172
  112.0 4.0 reshape.67
  116.1 2.7 copy.29
  124.2 2.1 slice_bitcast_fusion.9
  126.3 11.1 %collective-permute-done.3 = bf16[32,64,256]{2,1,0:T(8,128)(2,1)} collective-permute-done((bf16[32,64,256]{2,1,0:T(8,128)(2,1)}, bf16[32,64,256]{2,1,0:T(8,128)(2,1)}, u32[]{:S(2)}, u32[]{:S(2)}) %collective-permute-start.3) | collective-permute-done | bytes 1048608 | tf_op jit(solution)/shard_map/ppermute | solution.py:172
  137.4 2.1 slice_bitcast_fusion.12
  139.5 2.4 slice_bitcast_fusion.8
  143.0 2.9 collective-permute-done.19
  148.5 1.9 constant_dynamic-slice_fusion.2
  156.0 1.8 copy.54
  159.7 9.0 %collective-permute-done.20 = bf16[2,16,64,256]{3,2,1,0:T(8,128)(2,1)} collective-permute-done((bf16[2,16,64,256]{3,2,1,0:T(8,128)(2,1)}, bf16[2,16,64,256]{3,2,1,0:T(8,128)(2,1)}, u32[]{:S(2)}, u32[]{:S(2)}) %collective-permute-start.20) | collective-permute-done | bytes 1048608 | tf_op jit(solution)/shard_map/ppermute | solution.py:172
  170.3 1.8 slice_bitcast_fusion
  172.4 6.0 %collective-permute-done.23.refs_25_ = bf16[32,64,256]{2,1,0:T(8,128)(2,1)} collective-permute-done((bf16[32,64,256]{2,1,0:T(8,128)(2,1)}, bf16[32,64,256]{2,1,0:T(8,128)(2,1)}, u32[]{:S(2)}, u32[]{:S(2)}) %collective-permute-start.23) | collective-permute-done | bytes 1048608 | tf_op jit(solution)/shard_map/ppermute | solution.py:172
  180.6 16.2 %collective-permute-done.31.refs_25_ = bf16[32,64,256]{2,1,0:T(8,128)(2,1)S(1)} collective-permute-done((bf16[32,64,256]{2,1,0:T(8,128)(2,1)S(1)}, bf16[32,64,256]{2,1,0:T(8,128)(2,1)S(1)}, u32[]{:S(2)}, u32[]{:S(2)}) %collective-permute-start.31) | collective-permute-done | bytes 1048608 | tf_op jit(solution)/shard_map/ppermute | solution.py:172
  196.9 1.7 maximum_select_fusion.1
  198.6 1.9 collective-permute-start.26
  203.5 31.0 %ladder.6.refs_26_ = f32[32,64,256]{2,1,0:T(8,128)} custom-call(s32[16]{0:T(128)S(1)} %stack.136.which_ref, bf16[32,64,256]{2,1,0:T(8,128)(2,1)S(1)} %bitcast.125, bf16[32,64,256]{2,1,0:T(8,128)(2,1)} %collective-permute-done.4.refs_1_, bf16[32,64,256]{2,1,0:T(8,128)(2,1)} %collective-permute-done.12.refs_2_, bf16[32,64,256]{2,1,0:T(8,128)(2,1)S(1)} %copy-done.8, ...), custom_call_target="tpu_custom_call" | custom-call | flops 19327352832 | bytes 26214400 | tf_op jit(solution)/shard_map/ladder/pallas_call | solution.py:124
  235.2 4.7 %collective-permute-start.33 = (bf16[2,16,64,256]{3,2,1,0:T(8,128)(2,1)}, bf16[2,16,64,256]{3,2,1,0:T(8,128)(2,1)S(1)}, u32[]{:S(2)}, u32[]{:S(2)}) collective-permute-start(bf16[2,16,64,256]{3,2,1,0:T(8,128)(2,1)} %get-tuple-element.81), channel_id=1, source_target_pairs={{0,8},{1,9},{2,10},{3,11},{4,12},{5,13},{6,14},{7,15},{8,0},{9,1},... | collective-permute-start | bytes 3145736 | tf_op jit(solution)/shard_map/ppermute | solution.py:172
  241.6 31.1 %ladder.7.refs_26_ = f32[32,64,256]{2,1,0:T(8,128)} custom-call(s32[16]{0:T(128)S(1)} %stack.136.which_ref, bf16[32,64,256]{2,1,0:T(8,128)(2,1)S(1)} %bitcast.126, bf16[32,64,256]{2,1,0:T(8,128)(2,1)} %collective-permute-done.4.refs_1_, bf16[32,64,256]{2,1,0:T(8,128)(2,1)} %collective-permute-done.12.refs_2_, ...), custom_call_target="tpu_custom_call", output_to_operand_aliasing={{}: (27, {})} | custom-call | flops 19327352832 | bytes 26214400 | tf_op jit(solution)/shard_map/ladder/pallas_call | solution.py:124
  272.7 4.9 %collective-permute-start.38 = (bf16[2,16,64,256]{3,2,1,0:T(8,128)(2,1)}, bf16[2,16,64,256]{3,2,1,0:T(8,128)(2,1)S(1)}, u32[]{:S(2)}, u32[]{:S(2)}) collective-permute-start(bf16[2,16,64,256]{3,2,1,0:T(8,128)(2,1)} %get-tuple-element.86), channel_id=1, source_target_pairs={{0,8},{1,9},{2,10},{3,11},{4,12},{5,13},{6,14},{7,15},{8,0},{9,1},... | collective-permute-start | bytes 3145736 | tf_op jit(solution)/shard_map/ppermute | solution.py:172
  280.2 30.8 %ladder.8.refs_26_ = f32[32,64,256]{2,1,0:T(8,128)} custom-call(s32[16]{0:T(128)S(1)} %stack.136.which_ref, bf16[2,16,64,256]{3,2,1,0:T(8,128)(2,1)S(1)} %get-tuple-element.75.refs_0_.refs_1_, bf16[2,16,64,256]{3,2,1,0:T(8,128)(2,1)S(1)} %get-tuple-element.75.refs_0_.refs_1_, ...), custom_call_target="tpu_custom_call", output_to_operand_aliasing={{}: (27, {})} | custom-call | flops 19327352832 | bytes 26214400 | tf_op jit(solution)/shard_map/ladder/pallas_call | solution.py:124
  314.5 30.7 %ladder.9.refs_14_ = f32[32,64,256]{2,1,0:T(8,128)} custom-call(s32[16]{0:T(128)S(1)} %stack.136.which_ref, bf16[2,16,64,256]{3,2,1,0:T(8,128)(2,1)S(1)} %get-tuple-element.73.refs_0_.refs_1_, bf16[2,16,64,256]{3,2,1,0:T(8,128)(2,1)S(1)} %get-tuple-element.73.refs_0_.refs_1_, ...), custom_call_target="tpu_custom_call", output_to_operand_aliasing={{}: (27, {})} | custom-call | flops 19327352832 | bytes 26214400 | tf_op jit(solution)/shard_map/ladder/pallas_call | solution.py:124
  346.9 19.0 %ladder.10.refs_14_ = f32[32,64,256]{2,1,0:T(8,128)S(1)} custom-call(s32[8]{0:T(128)S(1)} %stack.126.which_ref, bf16[2,16,64,256]{3,2,1,0:T(8,128)(2,1)S(1)} %collective-permute-done.27.refs_4_.refs_5_.refs_0_.refs_1_, bf16[2,16,64,256]{3,2,1,0:T(8,128)(2,1)S(1)} %collective-permute-done.27.refs_4_.refs_5_.refs_0_.refs_1_, ...), custom_call_target="tpu_custom_call", output_to_operand_aliasing={{}: (15, {})} | custom-call | flops 10737418240 | bytes 15728640 | tf_op jit(solution)/shard_map/ladder/pallas_call | solution.py:124
  365.9 19.0 %ladder.11 = f32[32,64,256]{2,1,0:T(8,128)S(1)} custom-call(s32[8]{0:T(128)S(1)} %stack.126.which_ref, bf16[2,16,64,256]{3,2,1,0:T(8,128)(2,1)S(1)} %collective-permute-done.25.refs_4_.refs_5_.refs_0_.refs_1_, bf16[2,16,64,256]{3,2,1,0:T(8,128)(2,1)S(1)} %collective-permute-done.25.refs_4_.refs_5_.refs_0_.refs_1_, ...), custom_call_target="tpu_custom_call", output_to_operand_aliasing={{}: (15, {})} | custom-call | flops 10737418240 | bytes 15728640 | tf_op jit(solution)/shard_map/ladder/pallas_call | solution.py:124
  386.5 2.6 collective-permute-done.40
  393.1 7.2 %collective-permute-done.43 = f32[2,4,16,512]{3,2,1,0:T(8,128)S(1)} collective-permute-done((f32[2,4,16,512]{3,2,1,0:T(8,128)S(1)}, f32[2,4,16,512]{3,2,1,0:T(8,128)S(1)}, u32[]{:S(2)}, u32[]{:S(2)}) %collective-permute-start.43) | collective-permute-done | bytes 262176 | tf_op jit(solution)/shard_map/ppermute | solution.py:172
  402.3 3.1 collective-permute-done.44
  406.1 10.9 %collective-permute-start.45 = (f32[32,512]{1,0:T(8,128)S(1)}, f32[32,512]{1,0:T(8,128)S(1)}, u32[]{:S(2)}, u32[]{:S(2)}) collective-permute-start(f32[32,512]{1,0:T(8,128)S(1)} %get-tuple-element.92), channel_id=1, source_target_pairs={{0,8},{1,9},{2,10},{3,11},{4,12},{5,13},{6,14},{7,15},{8,0},{9,1},... | collective-permute-start | bytes 196616 | tf_op jit(solution)/shard_map/ppermute | solution.py:172
  417.5 2.0 collective-permute-start.47
  420.6 1.9 collective-permute-done.46
  (210 shorter events, 59.5 us)
Async XLA Ops:
  3.8 26.3 %collective-permute-start = (bf16[32,64,256]{2,1,0:T(8,128)(2,1)}, bf16[32,64,256]{2,1,0:T(8,128)(2,1)S(1)}, u32[]{:S(2)}, u32[]{:S(2)}) collective-permute-start(bf16[32,64,256]{2,1,0:T(8,128)(2,1)} %get-tuple-element.54.refs_8_), channel_id=1, source_target_pairs={{0,2},{1,3},{2,0},{3,1},{4,6},{5,7},{6,4},{7,5},{8,10},{9,11},{10,... | collective-permute-start | bytes 3145736 | tf_op jit(solution)/shard_map/ppermute | solution.py:172
  30.2 8.4 %collective-permute-start.14 = (bf16[32,64,256]{2,1,0:T(8,128)(2,1)S(1)}, bf16[32,64,256]{2,1,0:T(8,128)(2,1)S(1)}, u32[]{:S(2)}, u32[]{:S(2)}) collective-permute-start(bf16[32,64,256]{2,1,0:T(8,128)(2,1)S(1)} %bitcast.123), channel_id=1, source_target_pairs={{8,16},{9,17},{10,18},{11,19},{12,20},{13,21},{14,22},{15,23},{16,... | collective-permute-start | bytes 3145736 | tf_op jit(solution)/shard_map/ppermute | solution.py:172
  30.9 24.7 %collective-permute-start.4 = (bf16[32,64,256]{2,1,0:T(8,128)(2,1)}, bf16[32,64,256]{2,1,0:T(8,128)(2,1)}, u32[]{:S(2)}, u32[]{:S(2)}) collective-permute-start(bf16[32,64,256]{2,1,0:T(8,128)(2,1)} %bitcast.11), channel_id=1, source_target_pairs={{0,4},{1,5},{2,6},{3,7},{4,0},{5,1},{6,2},{7,3},{8,12},{9,13},{10,... | collective-permute-start | bytes 3145736 | tf_op jit(solution)/shard_map/ppermute | solution.py:172
  32.7 26.2 %collective-permute-start.12 = (bf16[32,64,256]{2,1,0:T(8,128)(2,1)S(1)}, bf16[32,64,256]{2,1,0:T(8,128)(2,1)}, u32[]{:S(2)}, u32[]{:S(2)}) collective-permute-start(bf16[32,64,256]{2,1,0:T(8,128)(2,1)S(1)} %bitcast.124), channel_id=1, source_target_pairs={{0,8},{1,9},{2,10},{3,11},{4,12},{5,13},{6,14},{7,15},{8,0},{9,1},... | collective-permute-start | bytes 3145736 | tf_op jit(solution)/shard_map/ppermute | solution.py:172
  37.0 27.0 %collective-permute-start.1 = (bf16[32,64,256]{2,1,0:T(8,128)(2,1)}, bf16[32,64,256]{2,1,0:T(8,128)(2,1)S(1)}, u32[]{:S(2)}, u32[]{:S(2)}) collective-permute-start(bf16[32,64,256]{2,1,0:T(8,128)(2,1)} %get-tuple-element.51.refs_9_), channel_id=1, source_target_pairs={{0,2},{1,3},{2,0},{3,1},{4,6},{5,7},{6,4},{7,5},{8,10},{9,11},{10,... | collective-permute-start | bytes 3145736 | tf_op jit(solution)/shard_map/ppermute | solution.py:172
  55.6 10.8 %collective-permute-start.15 = (bf16[32,64,256]{2,1,0:T(8,128)(2,1)}, bf16[32,64,256]{2,1,0:T(8,128)(2,1)}, u32[]{:S(2)}, u32[]{:S(2)}) collective-permute-start(bf16[32,64,256]{2,1,0:T(8,128)(2,1)} %collective-permute-done.4.refs_1_), channel_id=1, source_target_pairs={{8,16},{9,17},{10,18},{11,19},{12,20},{13,21},{14,22},{15,23},{16,... | collective-permute-start | bytes 3145736 | tf_op jit(solution)/shard_map/ppermute | solution.py:172
  57.2 34.1 %collective-permute-start.7 = (bf16[2,32,64,256]{3,2,1,0:T(8,128)(2,1)}, bf16[2,32,64,256]{3,2,1,0:T(8,128)(2,1)}, u32[]{:S(2)}, u32[]{:S(2)}) collective-permute-start(bf16[2,32,64,256]{3,2,1,0:T(8,128)(2,1)} %bitcast.133), channel_id=1, source_target_pairs={{0,1},{1,0},{2,3},{3,2},{4,5},{5,4},{6,7},{7,6},{8,9},{9,8},{10,11... | collective-permute-start | bytes 6291464 | tf_op jit(solution)/shard_map/ppermute | solution.py:172
  58.8 29.4 %collective-permute-start.13 = (bf16[32,64,256]{2,1,0:T(8,128)(2,1)}, bf16[32,64,256]{2,1,0:T(8,128)(2,1)S(1)}, u32[]{:S(2)}, u32[]{:S(2)}) collective-permute-start(bf16[32,64,256]{2,1,0:T(8,128)(2,1)} %collective-permute-done.4.refs_1_), channel_id=1, source_target_pairs={{0,8},{1,9},{2,10},{3,11},{4,12},{5,13},{6,14},{7,15},{8,0},{9,1},... | collective-permute-start | bytes 3145736 | tf_op jit(solution)/shard_map/ppermute | solution.py:172
  64.0 34.2 %collective-permute-start.2 = (bf16[32,64,256]{2,1,0:T(8,128)(2,1)}, bf16[32,64,256]{2,1,0:T(8,128)(2,1)}, u32[]{:S(2)}, u32[]{:S(2)}) collective-permute-start(bf16[32,64,256]{2,1,0:T(8,128)(2,1)} %get-tuple-element.51.refs_9_), channel_id=1, source_target_pairs={{0,4},{1,5},{2,6},{3,7},{4,0},{5,1},{6,2},{7,3},{8,12},{9,13},{10,... | collective-permute-start | bytes 3145736 | tf_op jit(solution)/shard_map/ppermute | solution.py:172
  69.8 40.6 %collective-permute-start.16 = (bf16[2,16,64,256]{3,2,1,0:T(8,128)(2,1)}, bf16[2,16,64,256]{3,2,1,0:T(8,128)(2,1)S(1)}, u32[]{:S(2)}, u32[]{:S(2)}) collective-permute-start(bf16[2,16,64,256]{3,2,1,0:T(8,128)(2,1)} %broadcast_select_fusion.9), channel_id=1, source_target_pairs={{0,8},{1,9},{2,10},{3,11},{4,12},{5,13},{6,14},{7,15},{8,0},{9,1},... | collective-permute-start | bytes 3145736 | tf_op jit(solution)/shard_map/ppermute | solution.py:172
  88.2 32.1 %collective-permute-start.17 = (bf16[32,64,256]{2,1,0:T(8,128)(2,1)}, bf16[32,64,256]{2,1,0:T(8,128)(2,1)}, u32[]{:S(2)}, u32[]{:S(2)}) collective-permute-start(bf16[32,64,256]{2,1,0:T(8,128)(2,1)} %collective-permute-done.12.refs_2_), channel_id=1, source_target_pairs={{8,16},{9,17},{10,18},{11,19},{12,20},{13,21},{14,22},{15,23},{16,... | collective-permute-start | bytes 3145736 | tf_op jit(solution)/shard_map/ppermute | solution.py:172
  89.9 32.9 %collective-permute-start.5 = (bf16[32,64,256]{2,1,0:T(8,128)(2,1)}, bf16[32,64,256]{2,1,0:T(8,128)(2,1)}, u32[]{:S(2)}, u32[]{:S(2)}) collective-permute-start(bf16[32,64,256]{2,1,0:T(8,128)(2,1)} %get-tuple-element.54.refs_8_), channel_id=1, source_target_pairs={{0,4},{1,5},{2,6},{3,7},{4,0},{5,1},{6,2},{7,3},{8,12},{9,13},{10,... | collective-permute-start | bytes 3145736 | tf_op jit(solution)/shard_map/ppermute | solution.py:172
  91.4 32.9 %collective-permute-start.8 = (bf16[32,64,256]{2,1,0:T(8,128)(2,1)S(1)}, bf16[32,64,256]{2,1,0:T(8,128)(2,1)}, u32[]{:S(2)}, u32[]{:S(2)}) collective-permute-start(bf16[32,64,256]{2,1,0:T(8,128)(2,1)S(1)} %collective-permute-done.refs_16_), channel_id=1, source_target_pairs={{0,1},{1,0},{2,3},{3,2},{4,5},{5,4},{6,7},{7,6},{8,9},{9,8},{10,11... | collective-permute-start | bytes 3145736 | tf_op jit(solution)/shard_map/ppermute | solution.py:172
  98.2 39.2 %collective-permute-start.3 = (bf16[32,64,256]{2,1,0:T(8,128)(2,1)}, bf16[32,64,256]{2,1,0:T(8,128)(2,1)}, u32[]{:S(2)}, u32[]{:S(2)}) collective-permute-start(bf16[32,64,256]{2,1,0:T(8,128)(2,1)} %bitcast.139), channel_id=1, source_target_pairs={{0,4},{1,5},{2,6},{3,7},{4,0},{5,1},{6,2},{7,3},{8,12},{9,13},{10,... | collective-permute-start | bytes 3145736 | tf_op jit(solution)/shard_map/ppermute | solution.py:172
  110.4 29.1 %collective-permute-start.18 = (bf16[32,64,256]{2,1,0:T(8,128)(2,1)}, bf16[32,64,256]{2,1,0:T(8,128)(2,1)}, u32[]{:S(2)}, u32[]{:S(2)}) collective-permute-start(bf16[32,64,256]{2,1,0:T(8,128)(2,1)} %copy-done.7), channel_id=1, source_target_pairs={{8,16},{9,17},{10,18},{11,19},{12,20},{13,21},{14,22},{15,23},{16,... | collective-permute-start | bytes 3145736 | tf_op jit(solution)/shard_map/ppermute | solution.py:172
  120.3 25.7 %collective-permute-start.19 = (bf16[2,16,64,256]{3,2,1,0:T(8,128)(2,1)S(1)}, bf16[2,16,64,256]{3,2,1,0:T(8,128)(2,1)S(1)}, u32[]{:S(2)}, u32[]{:S(2)}) collective-permute-start(bf16[2,16,64,256]{3,2,1,0:T(8,128)(2,1)S(1)} %pad_maximum_fusion.4), channel_id=1, source_target_pairs={{8,0},{9,1},{10,2},{11,3},{12,4},{13,5},{14,6},{15,7},{16,24},{17,... | collective-permute-start | bytes 3145736 | tf_op jit(solution)/shard_map/ppermute | solution.py:172
  122.7 23.9 %collective-permute-start.6 = (bf16[32,64,256]{2,1,0:T(8,128)(2,1)}, bf16[32,64,256]{2,1,0:T(8,128)(2,1)}, u32[]{:S(2)}, u32[]{:S(2)}) collective-permute-start(bf16[32,64,256]{2,1,0:T(8,128)(2,1)} %collective-permute-done.5.refs_10_), channel_id=1, source_target_pairs={{0,2},{1,3},{2,0},{3,1},{4,6},{5,7},{6,4},{7,5},{8,10},{9,11},{10,... | collective-permute-start | bytes 3145736 | tf_op jit(solution)/shard_map/ppermute | solution.py:172
  124.2 29.2 %collective-permute-start.9 = (bf16[32,64,256]{2,1,0:T(8,128)(2,1)S(1)}, bf16[32,64,256]{2,1,0:T(8,128)(2,1)S(1)}, u32[]{:S(2)}, u32[]{:S(2)}) collective-permute-start(bf16[32,64,256]{2,1,0:T(8,128)(2,1)S(1)} %copy-done.5), channel_id=1, source_target_pairs={{0,1},{1,0},{2,3},{3,2},{4,5},{5,4},{6,7},{7,6},{8,9},{9,8},{10,11... | collective-permute-start | bytes 3145736 | tf_op jit(solution)/shard_map/ppermute | solution.py:172
  146.0 22.7 %collective-permute-start.20 = (bf16[2,16,64,256]{3,2,1,0:T(8,128)(2,1)}, bf16[2,16,64,256]{3,2,1,0:T(8,128)(2,1)}, u32[]{:S(2)}, u32[]{:S(2)}) collective-permute-start(bf16[2,16,64,256]{3,2,1,0:T(8,128)(2,1)} %broadcast_select_fusion.7), channel_id=1, source_target_pairs={{0,8},{1,9},{2,10},{3,11},{4,12},{5,13},{6,14},{7,15},{8,0},{9,1},... | collective-permute-start | bytes 3145736 | tf_op jit(solution)/shard_map/ppermute | solution.py:172
  147.0 25.1 %collective-permute-start.21 = (bf16[32,64,256]{2,1,0:T(8,128)(2,1)}, bf16[32,64,256]{2,1,0:T(8,128)(2,1)}, u32[]{:S(2)}, u32[]{:S(2)}) collective-permute-start(bf16[32,64,256]{2,1,0:T(8,128)(2,1)} %collective-permute-done.2.refs_11_), channel_id=1, source_target_pairs={{0,2},{1,3},{2,0},{3,1},{4,6},{5,7},{6,4},{7,5},{8,10},{9,11},{10,... | collective-permute-start | bytes 3145736 | tf_op jit(solution)/shard_map/ppermute | solution.py:172
  151.9 26.4 %collective-permute-start.23 = (bf16[32,64,256]{2,1,0:T(8,128)(2,1)}, bf16[32,64,256]{2,1,0:T(8,128)(2,1)}, u32[]{:S(2)}, u32[]{:S(2)}) collective-permute-start(bf16[32,64,256]{2,1,0:T(8,128)(2,1)} %bitcast.116), channel_id=1, source_target_pairs={{0,4},{1,5},{2,6},{3,7},{4,0},{5,1},{6,2},{7,3},{8,12},{9,13},{10,... | collective-permute-start | bytes 3145736 | tf_op jit(solution)/shard_map/ppermute | solution.py:172
  154.4 24.0 %collective-permute-start.10 = (bf16[32,64,256]{2,1,0:T(8,128)(2,1)}, bf16[32,64,256]{2,1,0:T(8,128)(2,1)}, u32[]{:S(2)}, u32[]{:S(2)}) collective-permute-start(bf16[32,64,256]{2,1,0:T(8,128)(2,1)} %collective-permute-done.5.refs_10_), channel_id=1, source_target_pairs={{0,1},{1,0},{2,3},{3,2},{4,5},{5,4},{6,7},{7,6},{8,9},{9,8},{10,11... | collective-permute-start | bytes 3145736 | tf_op jit(solution)/shard_map/ppermute | solution.py:172
  168.7 28.1 %collective-permute-start.31 = (bf16[32,64,256]{2,1,0:T(8,128)(2,1)S(1)}, bf16[32,64,256]{2,1,0:T(8,128)(2,1)S(1)}, u32[]{:S(2)}, u32[]{:S(2)}) collective-permute-start(bf16[32,64,256]{2,1,0:T(8,128)(2,1)S(1)} %bitcast.142), channel_id=1, source_target_pairs={{0,4},{1,5},{2,6},{3,7},{4,0},{5,1},{6,2},{7,3},{8,12},{9,13},{10,... | collective-permute-start | bytes 3145736 | tf_op jit(solution)/shard_map/ppermute | solution.py:172
  172.1 26.5 %collective-permute-start.22 = (bf16[32,64,256]{2,1,0:T(8,128)(2,1)}, bf16[32,64,256]{2,1,0:T(8,128)(2,1)S(1)}, u32[]{:S(2)}, u32[]{:S(2)}) collective-permute-start(bf16[32,64,256]{2,1,0:T(8,128)(2,1)} %collective-permute-done.2.refs_11_), channel_id=1, source_target_pairs={{0,1},{1,0},{2,3},{3,2},{4,5},{5,4},{6,7},{7,6},{8,9},{9,8},{10,11... | collective-permute-start | bytes 3145736 | tf_op jit(solution)/shard_map/ppermute | solution.py:172
  178.4 24.2 %collective-permute-start.24 = (bf16[32,64,256]{2,1,0:T(8,128)(2,1)}, bf16[32,64,256]{2,1,0:T(8,128)(2,1)S(1)}, u32[]{:S(2)}, u32[]{:S(2)}) collective-permute-start(bf16[32,64,256]{2,1,0:T(8,128)(2,1)} %collective-permute-done.21.refs_19_), channel_id=1, source_target_pairs={{0,1},{1,0},{2,3},{3,2},{4,5},{5,4},{6,7},{7,6},{8,9},{9,8},{10,11... | collective-permute-start | bytes 3145736 | tf_op jit(solution)/shard_map/ppermute | solution.py:172
  178.4 24.2 %collective-permute-start.11 = (bf16[32,64,256]{2,1,0:T(8,128)(2,1)}, bf16[32,64,256]{2,1,0:T(8,128)(2,1)S(1)}, u32[]{:S(2)}, u32[]{:S(2)}) collective-permute-start(bf16[32,64,256]{2,1,0:T(8,128)(2,1)} %collective-permute-done.6.refs_18_), channel_id=1, source_target_pairs={{0,1},{1,0},{2,3},{3,2},{4,5},{5,4},{6,7},{7,6},{8,9},{9,8},{10,11... | collective-permute-start | bytes 3145736 | tf_op jit(solution)/shard_map/ppermute | solution.py:172
  198.6 42.1 %collective-permute-start.26 = (bf16[2,16,64,256]{3,2,1,0:T(8,128)(2,1)}, bf16[2,16,64,256]{3,2,1,0:T(8,128)(2,1)S(1)}, u32[]{:S(2)}, u32[]{:S(2)}) collective-permute-start(bf16[2,16,64,256]{3,2,1,0:T(8,128)(2,1)} %get-tuple-element.74), channel_id=1, source_target_pairs={{0,8},{1,9},{2,10},{3,11},{4,12},{5,13},{6,14},{7,15},{8,0},{9,1},... | collective-permute-start | bytes 3145736 | tf_op jit(solution)/shard_map/ppermute | solution.py:172
  201.7 39.0 %collective-permute-start.27 = (bf16[2,16,64,256]{3,2,1,0:T(8,128)(2,1)S(1)}, bf16[2,16,64,256]{3,2,1,0:T(8,128)(2,1)S(1)}, u32[]{:S(2)}, u32[]{:S(2)}) collective-permute-start(bf16[2,16,64,256]{3,2,1,0:T(8,128)(2,1)S(1)} %get-tuple-element.75.refs_0_.refs_1_), channel_id=1, source_target_pairs={{8,16},{9,17},{10,18},{11,19},{12,20},{13,21},{14,22},{15,23},{16,... | collective-permute-start | bytes 3145736 | tf_op jit(solution)/shard_map/ppermute | solution.py:172
  234.5 38.2 %collective-permute-start.25 = (bf16[2,16,64,256]{3,2,1,0:T(8,128)(2,1)S(1)}, bf16[2,16,64,256]{3,2,1,0:T(8,128)(2,1)S(1)}, u32[]{:S(2)}, u32[]{:S(2)}) collective-permute-start(bf16[2,16,64,256]{3,2,1,0:T(8,128)(2,1)S(1)} %get-tuple-element.73.refs_0_.refs_1_), channel_id=1, source_target_pairs={{8,16},{9,17},{10,18},{11,19},{12,20},{13,21},{14,22},{15,23},{16,... | collective-permute-start | bytes 3145736 | tf_op jit(solution)/shard_map/ppermute | solution.py:172
  235.2 42.4 %collective-permute-start.33 = (bf16[2,16,64,256]{3,2,1,0:T(8,128)(2,1)}, bf16[2,16,64,256]{3,2,1,0:T(8,128)(2,1)S(1)}, u32[]{:S(2)}, u32[]{:S(2)}) collective-permute-start(bf16[2,16,64,256]{3,2,1,0:T(8,128)(2,1)} %get-tuple-element.81), channel_id=1, source_target_pairs={{0,8},{1,9},{2,10},{3,11},{4,12},{5,13},{6,14},{7,15},{8,0},{9,1},... | collective-permute-start | bytes 3145736 | tf_op jit(solution)/shard_map/ppermute | solution.py:172
  240.0 37.7 %collective-permute-start.32 = (bf16[32,64,256]{2,1,0:T(8,128)(2,1)S(1)}, bf16[32,64,256]{2,1,0:T(8,128)(2,1)S(1)}, u32[]{:S(2)}, u32[]{:S(2)}) collective-permute-start(bf16[32,64,256]{2,1,0:T(8,128)(2,1)S(1)} %bitcast.127), channel_id=1, source_target_pairs={{8,12},{9,13},{10,14},{11,15},{12,8},{13,9},{14,10},{15,11},{16,20... | collective-permute-start | bytes 3145736 | tf_op jit(solution)/shard_map/ppermute | solution.py:172
  240.7 38.8 %collective-permute-start.28 = (bf16[2,16,64,256]{3,2,1,0:T(8,128)(2,1)}, bf16[2,16,64,256]{3,2,1,0:T(8,128)(2,1)S(1)}, u32[]{:S(2)}, u32[]{:S(2)}) collective-permute-start(bf16[2,16,64,256]{3,2,1,0:T(8,128)(2,1)} %collective-permute-done.20), channel_id=1, source_target_pairs={{8,16},{9,17},{10,18},{11,19},{12,20},{13,21},{14,22},{15,23},{16,... | collective-permute-start | bytes 3145736 | tf_op jit(solution)/shard_map/ppermute | solution.py:172
  272.7 38.3 %collective-permute-start.38 = (bf16[2,16,64,256]{3,2,1,0:T(8,128)(2,1)}, bf16[2,16,64,256]{3,2,1,0:T(8,128)(2,1)S(1)}, u32[]{:S(2)}, u32[]{:S(2)}) collective-permute-start(bf16[2,16,64,256]{3,2,1,0:T(8,128)(2,1)} %get-tuple-element.86), channel_id=1, source_target_pairs={{0,8},{1,9},{2,10},{3,11},{4,12},{5,13},{6,14},{7,15},{8,0},{9,1},... | collective-permute-start | bytes 3145736 | tf_op jit(solution)/shard_map/ppermute | solution.py:172
  277.7 33.4 %collective-permute-start.34 = (bf16[32,64,256]{2,1,0:T(8,128)(2,1)S(1)}, bf16[32,64,256]{2,1,0:T(8,128)(2,1)S(1)}, u32[]{:S(2)}, u32[]{:S(2)}) collective-permute-start(bf16[32,64,256]{2,1,0:T(8,128)(2,1)S(1)} %collective-permute-done.32.refs_6_), channel_id=1, source_target_pairs={{8,10},{9,11},{10,8},{11,9},{12,14},{13,15},{14,12},{15,13},{16,18... | collective-permute-start | bytes 3145736 | tf_op jit(solution)/shard_map/ppermute | solution.py:172
  278.4 32.7 %collective-permute-start.30 = (bf16[32,64,256]{2,1,0:T(8,128)(2,1)S(1)}, bf16[32,64,256]{2,1,0:T(8,128)(2,1)S(1)}, u32[]{:S(2)}, u32[]{:S(2)}) collective-permute-start(bf16[32,64,256]{2,1,0:T(8,128)(2,1)S(1)} %bitcast.128), channel_id=1, source_target_pairs={{8,10},{9,11},{10,8},{11,9},{12,14},{13,15},{14,12},{15,13},{16,18... | collective-permute-start | bytes 3145736 | tf_op jit(solution)/shard_map/ppermute | solution.py:172
  279.5 32.3 %collective-permute-start.29 = (bf16[2,16,64,256]{3,2,1,0:T(8,128)(2,1)S(1)}, bf16[2,16,64,256]{3,2,1,0:T(8,128)(2,1)S(1)}, u32[]{:S(2)}, u32[]{:S(2)}) collective-permute-start(bf16[2,16,64,256]{3,2,1,0:T(8,128)(2,1)S(1)} %collective-permute-done.26), channel_id=1, source_target_pairs={{8,16},{9,17},{10,18},{11,19},{12,20},{13,21},{14,22},{15,23},{16,... | collective-permute-start | bytes 3145736 | tf_op jit(solution)/shard_map/ppermute | solution.py:172
  311.0 34.2 %collective-permute-start.39 = (bf16[32,64,256]{2,1,0:T(8,128)(2,1)S(1)}, bf16[32,64,256]{2,1,0:T(8,128)(2,1)S(1)}, u32[]{:S(2)}, u32[]{:S(2)}) collective-permute-start(bf16[32,64,256]{2,1,0:T(8,128)(2,1)S(1)} %collective-permute-done.34.refs_7_), channel_id=1, source_target_pairs={{0,1},{1,0},{2,3},{3,2},{4,5},{5,4},{6,7},{7,6},{8,9},{9,8},{10,11... | collective-permute-start | bytes 3145736 | tf_op jit(solution)/shard_map/ppermute | solution.py:172
  311.1 34.1 %collective-permute-start.36 = (bf16[32,64,256]{2,1,0:T(8,128)(2,1)S(1)}, bf16[32,64,256]{2,1,0:T(8,128)(2,1)}, u32[]{:S(2)}, u32[]{:S(2)}) collective-permute-start(bf16[32,64,256]{2,1,0:T(8,128)(2,1)S(1)} %collective-permute-done.30.refs_5_), channel_id=1, source_target_pairs={{0,1},{1,0},{2,3},{3,2},{4,5},{5,4},{6,7},{7,6},{8,9},{9,8},{10,11... | collective-permute-start | bytes 3145736 | tf_op jit(solution)/shard_map/ppermute | solution.py:172
  311.6 33.6 %collective-permute-start.35 = (bf16[32,64,256]{2,1,0:T(8,128)(2,1)S(1)}, bf16[32,64,256]{2,1,0:T(8,128)(2,1)}, u32[]{:S(2)}, u32[]{:S(2)}) collective-permute-start(bf16[32,64,256]{2,1,0:T(8,128)(2,1)S(1)} %bitcast.129), channel_id=1, source_target_pairs={{0,1},{1,0},{2,3},{3,2},{4,5},{5,4},{6,7},{7,6},{8,9},{9,8},{10,11... | collective-permute-start | bytes 3145736 | tf_op jit(solution)/shard_map/ppermute | solution.py:172
  312.8 32.4 %collective-permute-start.37 = (bf16[32,64,256]{2,1,0:T(8,128)(2,1)S(1)}, bf16[32,64,256]{2,1,0:T(8,128)(2,1)}, u32[]{:S(2)}, u32[]{:S(2)}) collective-permute-start(bf16[32,64,256]{2,1,0:T(8,128)(2,1)S(1)} %collective-permute-done.32.refs_6_), channel_id=1, source_target_pairs={{0,1},{1,0},{2,3},{3,2},{4,5},{5,4},{6,7},{7,6},{8,9},{9,8},{10,11... | collective-permute-start | bytes 3145736 | tf_op jit(solution)/shard_map/ppermute | solution.py:172
  386.3 2.7 collective-permute-start.40
  391.9 8.4 %collective-permute-start.43 = (f32[2,4,16,512]{3,2,1,0:T(8,128)S(1)}, f32[2,4,16,512]{3,2,1,0:T(8,128)S(1)}, u32[]{:S(2)}, u32[]{:S(2)}) collective-permute-start(f32[2,4,16,512]{3,2,1,0:T(8,128)S(1)} %bitcast.143), channel_id=1, source_target_pairs={{0,2},{1,3},{2,0},{3,1},{4,6},{5,7},{6,4},{7,5},{8,10},{9,11},{10,... | collective-permute-start | bytes 786440 | tf_op jit(solution)/shard_map/ppermute | solution.py:172
  392.5 8.5 %collective-permute-start.41 = (f32[2,4,16,512]{3,2,1,0:T(8,128)S(1)}, f32[2,4,16,512]{3,2,1,0:T(8,128)S(1)}, u32[]{:S(2)}, u32[]{:S(2)}) collective-permute-start(f32[2,4,16,512]{3,2,1,0:T(8,128)S(1)} %dynamic-slice_bitcast_fusion.1), channel_id=1, source_target_pairs={{0,4},{1,5},{2,6},{3,7},{4,0},{5,1},{6,2},{7,3},{8,12},{9,13},{10,... | collective-permute-start | bytes 786440 | tf_op jit(solution)/shard_map/ppermute | solution.py:172
  400.4 5.0 %collective-permute-start.44 = (f32[4,16,512]{2,1,0:T(8,128)S(1)}, f32[4,16,512]{2,1,0:T(8,128)S(1)}, u32[]{:S(2)}, u32[]{:S(2)}) collective-permute-start(f32[4,16,512]{2,1,0:T(8,128)S(1)} %dynamic-slice_bitcast_fusion.2), channel_id=1, source_target_pairs={{0,4},{1,5},{2,6},{3,7},{4,0},{5,1},{6,2},{7,3},{8,12},{9,13},{10,... | collective-permute-start | bytes 393224 | tf_op jit(solution)/shard_map/ppermute | solution.py:172
  401.0 5.0 %collective-permute-start.42 = (f32[4,16,512]{2,1,0:T(8,128)S(1)}, f32[4,16,512]{2,1,0:T(8,128)S(1)}, u32[]{:S(2)}, u32[]{:S(2)}) collective-permute-start(f32[4,16,512]{2,1,0:T(8,128)S(1)} %dynamic-slice_bitcast_fusion.3), channel_id=1, source_target_pairs={{0,2},{1,3},{2,0},{3,1},{4,6},{5,7},{6,4},{7,5},{8,10},{9,11},{10,... | collective-permute-start | bytes 393224 | tf_op jit(solution)/shard_map/ppermute | solution.py:172
  406.1 14.5 %collective-permute-start.45 = (f32[32,512]{1,0:T(8,128)S(1)}, f32[32,512]{1,0:T(8,128)S(1)}, u32[]{:S(2)}, u32[]{:S(2)}) collective-permute-start(f32[32,512]{1,0:T(8,128)S(1)} %get-tuple-element.92), channel_id=1, source_target_pairs={{0,8},{1,9},{2,10},{3,11},{4,12},{5,13},{6,14},{7,15},{8,0},{9,1},... | collective-permute-start | bytes 196616 | tf_op jit(solution)/shard_map/ppermute | solution.py:172
  417.0 5.5 %collective-permute-start.46 = (f32[32,512]{1,0:T(8,128)S(1)}, f32[32,512]{1,0:T(8,128)S(1)}, u32[]{:S(2)}, u32[]{:S(2)}) collective-permute-start(f32[32,512]{1,0:T(8,128)S(1)} %get-tuple-element.93), channel_id=1, source_target_pairs={{0,16},{1,17},{2,18},{3,19},{4,20},{5,21},{6,22},{7,23},{8,24},{9,... | collective-permute-start | bytes 196616 | tf_op jit(solution)/shard_map/ppermute | solution.py:172
  417.5 6.2 %collective-permute-start.47 = (f32[32,512]{1,0:T(8,128)S(1)}, f32[32,512]{1,0:T(8,128)S(1)}, u32[]{:S(2)}, u32[]{:S(2)}) collective-permute-start(f32[32,512]{1,0:T(8,128)S(1)} %get-tuple-element.94), channel_id=1, source_target_pairs={{0,24},{1,25},{2,26},{3,27},{4,28},{5,29},{6,30},{7,31},{8,16},{9,... | collective-permute-start | bytes 196616 | tf_op jit(solution)/shard_map/ppermute | solution.py:172
  (49 other events, 477.8 us)

commit v3 on v2

--- a/solution.py
+++ b/solution.py
@@ -8,7 +8,6 @@
 from jax.sharding import PartitionSpec as P
 
 AXES = ("row", "col")
-IN_FLIGHT = 5
 
 
 def contract_aux(left_piece, right_piece):
@@ -42,37 +41,49 @@
     return ladder / denom
 
 
-def ladder_kernel(slots, n_left, first, which_ref, *refs):
+def ladder_kernel(slots, n_left, choices, places, first, which_ref, *refs):
     pieces, refs = refs[:slots], refs[slots:]
-    lefts, refs = refs[: 4 * n_left], refs[4 * n_left :]
+    lefts, refs = refs[: 4 * n_left * choices], refs[4 * n_left * choices :]
     amp_own_ref, amp_other_ref, *add_ref, out_ref, held, sems = refs
     depth, width_b, width_q = pieces[0].shape
     _, _, _, tile_a, _, chunk_c, _ = held.shape
     span = 2 * chunk_c
     step, steps = pl.program_id(0), pl.num_programs(0)
 
-    def copies(at, slot):
+    def copies(at, slot, choice=0):
         rows = pl.ds(pl.multiple_of(at * tile_a, tile_a), tile_a)
+
+        def source(n):
+            return lefts[n].at[rows] if places[n] is None else lefts[n].at[places[n], rows]
+
         return [
             pltpu.make_async_copy(
-                lefts[4 * r + 2 * s + h].at[rows], held.at[slot, r, h, :, s], sems.at[slot, r, s, h]
+                source(4 * (choice * n_left + r) + 2 * s + h),
+                held.at[slot, r, h, :, s],
+                sems.at[slot, r, s, h],
             )
             for r in range(n_left)
             for s in range(2)
             for h in range(2)
         ]
 
+    def start(at, slot):
+        for choice in range(choices):
+
+            @pl.when(which_ref[2 * slots] == choice)
+            def _():
+                for copy in copies(at, slot, choice):
+                    copy.start()
+
+    slot = lax.rem(step, 2)
+
     @pl.when(step == 0)
     def _():
-        for copy in copies(step, 0):
-            copy.start()
-
-    slot = lax.rem(step, 2)
+        start(step, 0)
 
     @pl.when(step + 1 < steps)
     def _():
-        for copy in copies(step + 1, 1 - slot):
-            copy.start()
+        start(step + 1, 1 - slot)
 
     for copy in copies(step, slot):
         copy.wait()
@@ -105,10 +116,12 @@
     out_ref[...] = out if first else add_ref[0][...] + out
 
 
-def add_ladder(pieces, which, lefts, amps, add, depth, tile_a=4):
-    slots, n_left = len(pieces), len(lefts) // 4
+def add_ladder(pieces, which, lefts, amps, add, depth, choices=1, tile_a=4):
+    slots, n_left = len(pieces), len(lefts) // 4 // choices
+    places = [v[1] if isinstance(v, tuple) else None for v in lefts]
+    lefts = [v[0] if isinstance(v, tuple) else v for v in lefts]
     width_b, width_q = pieces[0][0].shape[-2:]
-    width_a, chunk_c = lefts[0].shape[:2]
+    width_a, chunk_c = lefts[0].shape[-3:-1]
     pairs = amps[0][0].shape[-1]
 
     def chunk_of(array, at):
@@ -119,10 +132,10 @@
     out_spec = pl.BlockSpec((tile_a, width_b, pairs), lambda i, w: (i, 0, 0))
     products = depth * width_b * width_a * 2 * chunk_c * (slots * width_q + pairs)
     moved = 2 * depth * (slots * width_b * width_q + 2 * chunk_c * pairs)
-    moved += sum(2 * v.size for v in lefts) + 8 * width_a * width_b * pairs
+    moved += 8 * n_left * width_a * chunk_c * width_q + 8 * width_a * width_b * pairs
     more = () if add is None else (add,)
     return pl.pallas_call(
-        functools.partial(ladder_kernel, slots, n_left, add is None),
+        functools.partial(ladder_kernel, slots, n_left, choices, places, add is None),
         grid_spec=pltpu.PrefetchScalarGridSpec(
             num_scalar_prefetch=1,
             grid=(width_a // tile_a,),
@@ -154,8 +167,7 @@
     def inner(at):
         return at in (half - 1, half)
 
-    issued = []
-    latest = []
+    before = []
 
     def send(value, place):
         pairs = []
@@ -168,9 +180,15 @@
                             source = (at_z * 2 + at_x) * n_col + at_y * 2 + at_k
                             target = (to[0] * 2 + to[1]) * n_col + to[2] * 2 + to[3]
                             pairs.append((source, target))
-        value, *_ = lax.optimization_barrier((value, *issued[-IN_FLIGHT:][:1], *latest))
-        got = lax.ppermute(value, AXES, pairs)
-        issued.append(got)
+        return lax.ppermute(value, AXES, pairs)
+
+    def now(*values):
+        return lax.optimization_barrier((values, tuple(before)))[0]
+
+    def step(*transfers, beside=()):
+        values = now(*(value for value, _ in transfers))
+        got = [send(value, place) for value, (_, place) in zip(values, transfers)]
+        before[:] = [*got, *beside]
         return got
 
     def other_x(c, x, y, k):
@@ -205,105 +223,123 @@
     part_d = local_d // 4
     depth = part_d // 2
 
-    def right_part(at_x, part):
-        rows = lax.dynamic_slice_in_dim(right_factors, at_x * 2 * part_d + part * part_d, part_d)
+    def right_part(at_x, part, right=right_factors):
+        rows = lax.dynamic_slice_in_dim(right, at_x * 2 * part_d + part * part_d, part_d)
         return rows.reshape(part_d, -1, width_b).transpose(0, 2, 1)
 
-    def amp_part(at_x, part):
-        got = lax.dynamic_slice_in_dim(amplitudes, at_x * 2 * part_d + part * part_d, part_d, 1)
+    def amp_part(at_x, part, amp):
+        got = lax.dynamic_slice_in_dim(amp, at_x * 2 * part_d + part * part_d, part_d, 1)
         return got.transpose(1, 0, 2)
 
     def both(one, two, at):
         rows = slice(at * depth, (at + 1) * depth)
         return jnp.stack([one[rows], two[rows]])
 
-    def swap(inner_one, end_one):
-        return send(jnp.where(is_inner, inner_one, end_one.reshape(inner_one.shape)), near)
+    def either(inner_one, end_one):
+        return jnp.where(is_inner, inner_one, end_one.reshape(inner_one.shape)), near
 
     far_inner = jnp.where(z < half, half, half - 1)
     planes = (z, z ^ 1, far_inner, far_inner ^ 1)
-    which = jnp.stack([v for p in planes for v in (p ^ col, x, p ^ col, 1 - x)])
-    turn = at_far.astype(x.dtype)
-    which_end = jnp.stack(
-        [v for p in planes[2:] for v in ((p % 2) ^ core, x ^ turn, (p % 2) ^ core, 1 - x ^ turn)]
-    )
-
-    y_0 = send(mine[0], other_y)
-    x_full = send(right_part(1 - x, 0), other_x)
-    o_full = right_part(x, 0)
-    near_o = send(o_full, near)
-    far_o = send(o_full, across)
-    mine_k = send(mine, other_core)
-    y_1 = send(mine[1], other_y)
-    x_0 = send(mine[0], other_x)
-    near_x = send(x_full, near)
-    far_x = send(x_full, across)
-    yk_0 = send(y_0, other_core)
-    x_1 = send(mine[1], other_x)
-    xy_0 = send(x_0, other_y)
-    third_o = send(near_o, across)
-    far_full = [both(far_o, far_x, i) for i in range(2)]
-    e3 = swap(far_full[0], jnp.where(at_far, mine[1], y_0))
-    yk_1 = send(y_1, other_core)
-    x_split = send(right_part(1 - x, 1), other_x)
-    xy_1 = send(x_1, other_y)
-    e4 = send(far_full[1], outward)
-    third_x = send(near_x, across)
-    xk_0 = send(x_0, other_core)
-    amp_full = (amp_part(x, 0), send(amp_part(1 - x, 0), other_x))
-    xk_1 = send(x_1, other_core)
-    o_split = right_part(x, 1)
-    split = [both(o_split, x_split, i) for i in range(2)]
+    which = jnp.stack([v for p in planes for v in (p ^ col, x, p ^ col, 1 - x)] + [jnp.zeros_like(x)])
+    turn = jnp.where(is_inner & at_far, 1, 0)
+    choice = jnp.where(is_inner, 0, jnp.where(at_far, 1, 2))
+    which_far = [v for p in planes[2:] for v in ((p % 2) ^ core, x ^ turn, (p % 2) ^ core, 1 - x ^ turn)]
+    which_far = jnp.stack(which_far + [choice])
+
+    mine, x_give, o_full = lax.optimization_barrier((mine, right_part(1 - x, 0), right_part(x, 0)))
+    before[:] = [x_give, o_full]
+    (right_later,) = now(right_factors)
+    near_o, far_o, x_full, y_0 = step(
+        (o_full, near), (o_full, across), (x_give, other_x), (mine[0], other_y)
+    )
+    give_split, o_split = right_part(1 - x, 1, right_later), right_part(x, 1, right_later)
+    before += [give_split, o_split]
+
+    (amp_later,) = now(amplitudes)
+    out_o, far_x, x_0, y_1, mine_k = step(
+        either(far_o, jnp.where(at_far, mine[1], y_0)),
+        (x_full, across),
+        (mine[0], other_x),
+        (mine[1], other_y),
+        (mine, other_core),
+    )
+    amp_full, amp_give = amp_part(x, 0, amp_later), amp_part(1 - x, 0, amp_later)
+    amp_own, amp_late = amp_part(x, 1, amp_later), amp_part(1 - x, 1, amp_later)
+    mixed = [both(give_split, amp_give, i) for i in range(2)]
+    before += [amp_full, amp_own, amp_late, *mixed]
+
+    near_x, third_o, x_1, xy_0, first_k = step(
+        (x_full, near),
+        (near_o, across),
+        (mine[1], other_x),
+        (x_0, other_y),
+        (jnp.stack([y_0, y_1, x_0]), other_core),
+    )
+    out_x, third_x, mixed[0], xy_1, second_k = step(
+        either(far_x, jnp.where(at_far, x_1, xy_0)),
+        (near_x, across),
+        (mixed[0], other_x),
+        (x_1, other_y),
+        (jnp.stack([x_1, xy_0]), other_core),
+    )
+    split = [jnp.stack([o_split[:depth], mixed[0][0]])]
+    beside, far_split, third_split = [None, None], [None, None], [None, None]
+    beside[0], far_split[0], mixed[1], end_y, xy_k = step(
+        (split[0], near),
+        (split[0], across),
+        (mixed[1], other_x),
+        (out_o, between_inner(other_y)),
+        (xy_1, other_core),
+    )
+    lefts = (mine[0], mine[1], x_0, x_1, mine_k[0], mine_k[1], (first_k, 2), (second_k, 0))
+    lefts += (y_0, y_1, xy_0, xy_1, (first_k, 0), (first_k, 1), (second_k, 1), xy_k)
+
+    def full(i, total):
+        pieces = [(v, i) for v in (o_full, x_full, near_o, near_x, far_o, far_x, third_o, third_x)]
+        return add_ladder(pieces, which, lefts, [(amp_full, i), (mixed[i], 1)], total, depth)
+
+    def parted(i, total):
+        pieces = [(v, h) for v in (split[i], beside[i], far_split[i], third_split[i]) for h in range(2)]
+        return add_ladder(pieces, which, lefts, [(v, i) for v in amp_split], total, depth)
+
+    def far_half(i, from_near, total):
+        far = jnp.where(is_inner, far_split[i], both(out_o, out_x, i))
+        third = jnp.where(is_inner, third_split[i], from_near)
+        amp = jnp.stack([amp_full[i * depth : (i + 1) * depth], mixed[i][1]])
+        amp = jnp.where(is_inner, from_near, amp)
+        pieces = [(v, h) for v in (far, third) for h in range(2)]
+        sets = (*ends, *lefts)
+        return add_ladder(pieces, which_far, sets, [(amp, 0), (amp, 1)], total, depth, choices=3)
+
+    total = full(0, None)
+    before.append(total)
+    split.append(jnp.stack([o_split[depth:], mixed[1][0]]))
+    beside[1], third_split[0], amp_late, end_xy, end_k = step(
+        (split[1], near),
+        (beside[0], across),
+        (amp_late, other_x),
+        (out_x, between_inner(other_y)),
+        (jnp.stack([out_o, out_x]), other_core),
+    )
+    amp_split = amp_own, amp_late
+    total = full(1, total)
+    before.append(total)
+    amp_both = [both(*now(*amp_split), i) for i in range(2)]
     third_full = [both(third_o, third_x, i) for i in range(2)]
-    far_split, third_split = [None, None], [None, None]
-    e5 = swap(third_full[0], split[0])
-    far_split[0] = send(split[0], across)
-    xyk_0 = send(xy_0, other_core)
-    xyk_1 = send(xy_1, other_core)
-    e6 = swap(third_full[1], split[1])
-    amp_split = (amp_part(x, 1), send(amp_part(1 - x, 1), other_x))
-    third_split[0] = send(e5, across)
-    lefts = (mine[0], mine[1], x_0, x_1, mine_k[0], mine_k[1], xk_0, xk_1)
-    lefts += (y_0, y_1, xy_0, xy_1, yk_0, yk_1, xyk_0, xyk_1)
-
-    def full(i, out_far, out_third, total):
-        far = jnp.where(is_inner, far_full[i], out_far)
-        third = jnp.where(is_inner, third_full[i], out_third)
-        pieces = [(o_full, i), (x_full, i), (near_o, i), (near_x, i)]
-        pieces += [(far, 0), (far, 1), (third, 0), (third, 1)]
-        return add_ladder(pieces, which, lefts, [(v, i) for v in amp_full], total, depth)
-
-    def parted(i, e_in, e_out, total):
-        beside = jnp.where(is_inner, e_in, e_out)
-        pieces = [(v, h) for v in (split[i], beside, far_split[i], third_split[i]) for h in range(2)]
-        return add_ladder(pieces, which, lefts, [(v, i) for v in amp_split], total, depth)
-
-    def ended(i, amp_end, total):
-        pieces = [(v, h) for v in (far_split[i], third_split[i]) for h in range(2)]
-        return add_ladder(pieces, which_end, ends, [(amp_end, 0), (amp_end, 1)], total, depth)
-
-    total = full(0, e3, e5, None)
-    latest[:] = [total]
-    far_split[1] = send(split[1], across)
-    amp_both = [both(*amp_split, i) for i in range(2)]
-    e7 = swap(split[0], amp_both[0])
-    end_own = e3.reshape(y_0.shape)
-    end_y = send(end_own, between_inner(other_y))
-    end_x = send(end_own, between_inner(other_x))
-    total = full(1, e4, e6, total)
-    latest[:] = [total]
-    third_split[1] = send(e6, across)
-    e8 = swap(split[1], amp_both[1])
-    end_xy = send(end_x, between_inner(other_y))
-    ends = (end_own, end_y, end_x, end_xy)
-    total = parted(0, e5, e7, total)
-    latest[:] = [total]
-    ends += tuple(send(v, other_core) for v in ends)
-    total = parted(1, e6, e8, total)
-    total = ended(0, e7, total)
-    total = ended(1, e8, total)
-    latest[:] = []
-    issued[:] = []
+    e7, far_split[1], end_yk = step(
+        either(third_full[0], amp_both[0]),
+        (split[1], across),
+        (jnp.stack([end_y, end_xy]), other_core),
+    )
+    total = parted(0, total)
+    before.append(total)
+    e8, third_split[1] = step(either(third_full[1], amp_both[1]), (beside[1], across))
+    ends = (out_o, end_y, out_x, end_xy, (end_k, 0), (end_yk, 0), (end_k, 1), (end_yk, 1))
+    total = far_half(0, e7, total)
+    before.append(total)
+    (e8,) = now(e8)
+    total = parted(1, total)
+    total = far_half(1, e8, total)
 
     def pick(value, at):
         return lax.dynamic_index_in_dim(value, at, 0, keepdims=False)

time: 426 us -> 389 us (0.913)
  starting transfers between devices: 85.7 us -> 57.8 us
  waiting for transfers between devices: 100 us -> 89.6 us
  local copies, waits for them, and re-layouts: 63.7 us -> 58.2 us
  other arithmetic: 12.5 us -> 17.6 us
    ppermute x48 -> x42, starting transfers between devices: 85.7 us -> 57.8 us  [send(): return lax.ppermute(value, AXES, pairs)]
    ppermute x48 -> x42, waiting for transfers between devices: 100 us -> 89.6 us  [send(): return lax.ppermute(value, AXES, pairs)]
    unnamed x102 -> x130, local copies, waits for them, and re-layouts: 15.3 us -> 6.43 us
    another operation x0 -> x6, other arithmetic: none -> 6.63 us  [the longest x1 3.12 us: by_lines(): jnp.stack([x_1, xy_0])]
    optimization_barrier x0 -> x1, local copies, waits for them, and re-layouts: none -> 4.56 us  [now(): return lax.optimization_barrier((values, tuple(before)))[0]]
    select_n x11 -> x8, other arithmetic: 8.71 us -> 7.03 us  [the longest x4 5.01 us: either(): jnp.where(is_inner, inner_one, end_one.reshape(inner_one.shape))]
  transfers between devices with their start and end apart: 48 -> 42, of which waited for: 18 -> 18; matrix products, arithmetic and copies ran while one was open for 14% -> 13% of each run, Pallas kernels for 29% -> 29%
where the time goes in v3:
time: 389 us; the launch traced here: 388 us
  Pallas kernels  163 us (42%)
  waiting for transfers between devices  89.6 us (23%)
  local copies, waits for them, and re-layouts  58.2 us (15%)
  starting transfers between devices  57.8 us (15%)
  other arithmetic  17.6 us (5%)
    pallas_call x6, Pallas kernels, add_ladder(): pl.pallas_call(functools.partial(ladder_kernel, slots, n_left, choices, p...  163 us
    ppermute x42, waiting for transfers between devices, send(): return lax.ppermute(value, AXES, pairs)  89.6 us
    ppermute x42, starting transfers between devices, send(): return lax.ppermute(value, AXES, pairs)  57.8 us
    reshape x8, local copies, waits for them, and re-layouts, right_part(): return rows.reshape(part_d, -1, width_b).transpose(0, 2, 1)  22 us
  transfers between devices with their start and end apart: 42, of which 18 were waited for; matrix products, arithmetic and copies ran while one was open for 13% of the time, Pallas kernels for 29%

profile of v3, /device:TPU:0, one launch (start us, length us, event | category | flops | bytes accessed | tf_op | source)
XLA Modules:
  0.0 387.6 jit_solution(14820246275849368827)
XLA Ops:
  0.0 2.7 constant_dynamic-slice_fusion.4
  2.7 3.0 reshape.62
  5.7 1.6 copy.30
  7.4 2.3 reshape.63
  11.3 1.9 copy.45
  14.4 2.9 collective-permute-start
  19.0 1.7 collective-permute-start.2
  22.2 3.0 constant_dynamic-slice_fusion.2
  25.2 4.0 %reshape.64 = bf16[32,256,64]{2,1,0:T(8,128)(2,1)} reshape(bf16[32,16384]{1,0:T(8,128)(2,1)} %get-tuple-element.94) | data formatting | bytes 2097152 | tf_op jit(solution)/shard_map/reshape | solution.py:228
  29.2 2.7 copy.32
  31.9 4.0 %reshape.65 = bf16[32,256,64]{2,1,0:T(8,128)(2,1)} reshape(bf16[32,16384]{1,0:T(8,128)(2,1)} %get-tuple-element.93) | data formatting | bytes 2097152 | tf_op jit(solution)/shard_map/reshape | solution.py:228
  36.0 2.7 copy.33
  38.7 6.3 %collective-permute-done.3.refs_16_.refs_20_ = bf16[32,64,256]{2,1,0:T(8,128)(2,1)S(1)} collective-permute-done((bf16[32,64,256]{2,1,0:T(8,128)(2,1)S(1)}, bf16[32,64,256]{2,1,0:T(8,128)(2,1)S(1)}, u32[]{:S(2)}, u32[]{:S(2)}) %collective-permute-start.3) | collective-permute-done | bytes 1048608 | tf_op jit(solution)/shard_map/ppermute | solution.py:183
  48.6 3.5 collective-permute-start.6
  52.9 4.6 %copy.34 = bf16[64,128,256]{2,0,1:T(8,128)(2,1)S(1)} copy(bf16[64,128,256]{2,1,0:T(8,128)(2,1)} %param.8) | data formatting | bytes 8388608 | tf_op jit(solution)/shard_map/optimization_barrier | solution.py:186
  57.5 1.8 dynamic-slice_bitcast_fusion.1
  60.8 11.2 %collective-permute-done.5.refs_17_.refs_21_ = bf16[32,64,256]{2,1,0:T(8,128)(2,1)S(1)} collective-permute-done((bf16[32,64,256]{2,1,0:T(8,128)(2,1)S(1)}, bf16[32,64,256]{2,1,0:T(8,128)(2,1)S(1)}, u32[]{:S(2)}, u32[]{:S(2)}) %collective-permute-start.5) | collective-permute-done | bytes 1048608 | tf_op jit(solution)/shard_map/ppermute | solution.py:183
  77.4 3.8 collective-permute-start.12
  82.0 19.1 %collective-permute-done.10.refs_11_.refs_15_ = bf16[32,64,256]{2,1,0:T(8,128)(2,1)} collective-permute-done((bf16[32,64,256]{2,1,0:T(8,128)(2,1)S(1)}, bf16[32,64,256]{2,1,0:T(8,128)(2,1)}, u32[]{:S(2)}, u32[]{:S(2)}) %collective-permute-start.10) | collective-permute-done | bytes 1048608 | tf_op jit(solution)/shard_map/ppermute | solution.py:183
  102.2 3.1 pad_maximum_fusion.1
  107.5 1.7 copy-done.41
  109.8 1.6 collective-permute-start.14
  111.4 1.8 collective-permute-start.16
  113.2 4.4 %collective-permute-start.17 = (bf16[32,64,256]{2,1,0:T(8,128)(2,1)}, bf16[32,64,256]{2,1,0:T(8,128)(2,1)}, u32[]{:S(2)}, u32[]{:S(2)}) collective-permute-start(bf16[32,64,256]{2,1,0:T(8,128)(2,1)} %select_select_fusion), channel_id=1, source_target_pairs={{0,8},{1,9},{2,10},{3,11},{4,12},{5,13},{6,14},{7,15},{8,0},{9,1},... | collective-permute-start | bytes 3145736 | tf_op jit(solution)/shard_map/ppermute | solution.py:183
  118.9 2.4 slice_bitcast_fusion.4
  122.2 12.9 %collective-permute-done.15.refs_25_ = bf16[2,16,64,256]{3,2,1,0:T(8,128)(2,1)} collective-permute-done((bf16[2,16,64,256]{3,2,1,0:T(8,128)(2,1)}, bf16[2,16,64,256]{3,2,1,0:T(8,128)(2,1)}, u32[]{:S(2)}, u32[]{:S(2)}) %collective-permute-start.15) | collective-permute-done | bytes 1048608 | tf_op jit(solution)/shard_map/ppermute | solution.py:183
  135.1 2.1 fusion.13
  137.3 3.9 collective-permute-done.17.refs_6_
  144.2 2.8 pad_maximum_fusion.2
  147.0 2.4 slice_bitcast_fusion.8
  149.4 2.2 slice_bitcast_fusion.6
  151.7 1.8 collective-permute-start.20
  154.9 10.8 %collective-permute-done.19.refs_25_ = bf16[2,16,64,256]{3,2,1,0:T(8,128)(2,1)S(1)} collective-permute-done((bf16[2,16,64,256]{3,2,1,0:T(8,128)(2,1)S(1)}, bf16[2,16,64,256]{3,2,1,0:T(8,128)(2,1)S(1)}, u32[]{:S(2)}, u32[]{:S(2)}) %collective-permute-start.19) | collective-permute-done | bytes 1048608 | tf_op jit(solution)/shard_map/ppermute | solution.py:183
  167.1 32.1 %ladder.6.refs_26_ = f32[32,64,256]{2,1,0:T(8,128)} custom-call(s32[17]{0:T(128)S(1)} %stack.223.which_ref, bf16[32,64,256]{2,1,0:T(8,128)(2,1)} %bitcast.7.refs_0_, bf16[32,64,256]{2,1,0:T(8,128)(2,1)} %collective-permute-done.refs_1_, bf16[32,64,256]{2,1,0:T(8,128)(2,1)} %collective-permute-done.1.refs_2_, ...), custom_call_target="tpu_custom_call" | custom-call | flops 19327352832 | bytes 26214400 | tf_op jit(solution)/shard_map/ladder/pallas_call | solution.py:137
  201.8 3.9 %collective-permute-start.25 = (bf16[2,16,64,256]{3,2,1,0:T(8,128)(2,1)S(1)}, bf16[2,16,64,256]{3,2,1,0:T(8,128)(2,1)}, u32[]{:S(2)}, u32[]{:S(2)}) collective-permute-start(bf16[2,16,64,256]{3,2,1,0:T(8,128)(2,1)S(1)} %pad_maximum_fusion.7.refs_0_.refs_1_), channel_id=1, source_target_pairs={{0,8},{1,9},{2,10},{3,11},{4,12},{5,13},{6,14},{7,15},{8,0},{9,1},... | collective-permute-start | bytes 3145736 | tf_op jit(solution)/shard_map/ppermute | solution.py:183
  206.5 32.0 %ladder.7.refs_26_ = f32[32,64,256]{2,1,0:T(8,128)} custom-call(s32[17]{0:T(128)S(1)} %stack.223.which_ref, bf16[32,64,256]{2,1,0:T(8,128)(2,1)} %bitcast.7.refs_0_, bf16[32,64,256]{2,1,0:T(8,128)(2,1)} %collective-permute-done.refs_1_, bf16[32,64,256]{2,1,0:T(8,128)(2,1)} %collective-permute-done.1.refs_2_, ...), custom_call_target="tpu_custom_call", output_to_operand_aliasing={{}: (27, {})} | custom-call | flops 19327352832 | bytes 26214400 | tf_op jit(solution)/shard_map/ladder/pallas_call | solution.py:137
  242.5 1.8 collective-permute-start.30
  245.1 29.8 %ladder.8.refs_30_ = f32[32,64,256]{2,1,0:T(8,128)S(1)} custom-call(s32[17]{0:T(128)S(1)} %stack.223.which_ref, bf16[2,16,64,256]{3,2,1,0:T(8,128)(2,1)S(1)} %pad_maximum_fusion.6.refs_0_.refs_1_, bf16[2,16,64,256]{3,2,1,0:T(8,128)(2,1)S(1)} %pad_maximum_fusion.6.refs_0_.refs_1_, ...), custom_call_target="tpu_custom_call", output_to_operand_aliasing={{}: (27, {})} | custom-call | flops 19327352832 | bytes 26214400 | tf_op jit(solution)/shard_map/ladder/pallas_call | solution.py:137
  279.0 5.0 %collective-permute-start.33 = (bf16[2,16,64,256]{3,2,1,0:T(8,128)(2,1)}, bf16[2,16,64,256]{3,2,1,0:T(8,128)(2,1)S(1)}, u32[]{:S(2)}, u32[]{:S(2)}) collective-permute-start(bf16[2,16,64,256]{3,2,1,0:T(8,128)(2,1)} %maximum_select_fusion.2), channel_id=1, source_target_pairs={{0,8},{1,9},{2,10},{3,11},{4,12},{5,13},{6,14},{7,15},{8,0},{9,1},... | collective-permute-start | bytes 3145736 | tf_op jit(solution)/shard_map/ppermute | solution.py:183
  284.2 19.4 %ladder.9.refs_26_ = f32[32,64,256]{2,1,0:T(8,128)S(1)} custom-call(s32[9]{0:T(128)S(1)} %stack.193.which_ref, bf16[2,16,64,256]{3,2,1,0:T(8,128)(2,1)S(1)} %maximum_select_fusion.3.refs_0_.refs_1_, bf16[2,16,64,256]{3,2,1,0:T(8,128)(2,1)S(1)} %maximum_select_fusion.3.refs_0_.refs_1_, ...), custom_call_target="tpu_custom_call", output_to_operand_aliasing={{}: (31, {})} | custom-call | flops 10737418240 | bytes 15728640 | tf_op jit(solution)/shard_map/ladder/pallas_call | solution.py:137
  303.7 3.6 collective-permute-done.33
  307.3 31.0 %ladder.10.refs_30_ = f32[32,64,256]{2,1,0:T(8,128)S(1)} custom-call(s32[17]{0:T(128)S(1)} %stack.223.which_ref, bf16[2,16,64,256]{3,2,1,0:T(8,128)(2,1)S(1)} %pad_maximum_fusion.7.refs_0_.refs_1_, bf16[2,16,64,256]{3,2,1,0:T(8,128)(2,1)S(1)} %pad_maximum_fusion.7.refs_0_.refs_1_, ...), custom_call_target="tpu_custom_call", output_to_operand_aliasing={{}: (27, {})} | custom-call | flops 19327352832 | bytes 26214400 | tf_op jit(solution)/shard_map/ladder/pallas_call | solution.py:137
  338.5 19.0 %ladder.11 = f32[32,64,256]{2,1,0:T(8,128)S(1)} custom-call(s32[9]{0:T(128)S(1)} %stack.193.which_ref, bf16[2,16,64,256]{3,2,1,0:T(8,128)(2,1)S(1)} %maximum_select_fusion.1.refs_0_.refs_1_, bf16[2,16,64,256]{3,2,1,0:T(8,128)(2,1)S(1)} %maximum_select_fusion.1.refs_0_.refs_1_, ...), custom_call_target="tpu_custom_call", output_to_operand_aliasing={{}: (31, {})} | custom-call | flops 10737418240 | bytes 15728640 | tf_op jit(solution)/shard_map/ladder/pallas_call | solution.py:137
  357.7 2.8 collective-permute-done.34
  365.5 6.3 %collective-permute-done.37 = f32[2,4,16,512]{3,2,1,0:T(8,128)S(1)} collective-permute-done((f32[2,4,16,512]{3,2,1,0:T(8,128)S(1)}, f32[2,4,16,512]{3,2,1,0:T(8,128)S(1)}, u32[]{:S(2)}, u32[]{:S(2)}) %collective-permute-start.37) | collective-permute-done | bytes 262176 | tf_op jit(solution)/shard_map/ppermute | solution.py:183
  374.0 2.9 collective-permute-done.38
  380.5 2.1 collective-permute-start.41
  383.4 1.9 collective-permute-done.40
  (235 shorter events, 56.1 us)
Async XLA Ops:
  14.4 60.9 %copy-start.8 = (bf16[32,64,256]{2,1,0:T(8,128)(2,1)}, bf16[32,64,256]{2,1,0:T(8,128)(2,1)S(1)}, u32[]{:S(2)}) copy-start(bf16[32,64,256]{2,1,0:T(8,128)(2,1)S(1)} %get-tuple-element.62.refs_9_.refs_13_) | copy-start | bytes 3145732
  14.4 31.9 %collective-permute-start = (bf16[32,64,256]{2,1,0:T(8,128)(2,1)}, bf16[32,64,256]{2,1,0:T(8,128)(2,1)}, u32[]{:S(2)}, u32[]{:S(2)}) collective-permute-start(bf16[32,64,256]{2,1,0:T(8,128)(2,1)} %bitcast.6), channel_id=1, source_target_pairs={{0,4},{1,5},{2,6},{3,7},{4,0},{5,1},{6,2},{7,3},{8,12},{9,13},{10,... | collective-permute-start | bytes 3145736 | tf_op jit(solution)/shard_map/ppermute | solution.py:183
  17.4 29.0 %collective-permute-start.1 = (bf16[32,64,256]{2,1,0:T(8,128)(2,1)}, bf16[32,64,256]{2,1,0:T(8,128)(2,1)}, u32[]{:S(2)}, u32[]{:S(2)}) collective-permute-start(bf16[32,64,256]{2,1,0:T(8,128)(2,1)} %bitcast.7.refs_0_), channel_id=1, source_target_pairs={{0,8},{1,9},{2,10},{3,11},{4,12},{5,13},{6,14},{7,15},{8,0},{9,1},... | collective-permute-start | bytes 3145736 | tf_op jit(solution)/shard_map/ppermute | solution.py:183
  19.0 19.7 %collective-permute-start.2 = (bf16[32,64,256]{2,1,0:T(8,128)(2,1)}, bf16[32,64,256]{2,1,0:T(8,128)(2,1)}, u32[]{:S(2)}, u32[]{:S(2)}) collective-permute-start(bf16[32,64,256]{2,1,0:T(8,128)(2,1)} %bitcast.7.refs_0_), channel_id=1, source_target_pairs={{8,16},{9,17},{10,18},{11,19},{12,20},{13,21},{14,22},{15,23},{16,... | collective-permute-start | bytes 3145736 | tf_op jit(solution)/shard_map/ppermute | solution.py:183
  20.7 24.3 %collective-permute-start.3 = (bf16[32,64,256]{2,1,0:T(8,128)(2,1)S(1)}, bf16[32,64,256]{2,1,0:T(8,128)(2,1)S(1)}, u32[]{:S(2)}, u32[]{:S(2)}) collective-permute-start(bf16[32,64,256]{2,1,0:T(8,128)(2,1)S(1)} %get-tuple-element.55.refs_8_.refs_12_), channel_id=1, source_target_pairs={{0,2},{1,3},{2,0},{3,1},{4,6},{5,7},{6,4},{7,5},{8,10},{9,11},{10,... | collective-permute-start | bytes 3145736 | tf_op jit(solution)/shard_map/ppermute | solution.py:183
  46.4 28.9 %collective-permute-start.8 = (bf16[2,32,64,256]{3,2,1,0:T(8,128)(2,1)S(1)}, bf16[2,32,64,256]{3,2,1,0:T(8,128)(2,1)S(1)}, u32[]{:S(2)}, u32[]{:S(2)}) collective-permute-start(bf16[2,32,64,256]{3,2,1,0:T(8,128)(2,1)S(1)} %bitcast.141), channel_id=1, source_target_pairs={{0,1},{1,0},{2,3},{3,2},{4,5},{5,4},{6,7},{7,6},{8,9},{9,8},{10,11... | collective-permute-start | bytes 6291464 | tf_op jit(solution)/shard_map/ppermute | solution.py:183
  46.5 25.6 %collective-permute-start.5 = (bf16[32,64,256]{2,1,0:T(8,128)(2,1)S(1)}, bf16[32,64,256]{2,1,0:T(8,128)(2,1)S(1)}, u32[]{:S(2)}, u32[]{:S(2)}) collective-permute-start(bf16[32,64,256]{2,1,0:T(8,128)(2,1)S(1)} %get-tuple-element.62.refs_9_.refs_13_), channel_id=1, source_target_pairs={{0,2},{1,3},{2,0},{3,1},{4,6},{5,7},{6,4},{7,5},{8,10},{9,11},{10,... | collective-permute-start | bytes 3145736 | tf_op jit(solution)/shard_map/ppermute | solution.py:183
  48.1 25.2 %collective-permute-start.4 = (bf16[32,64,256]{2,1,0:T(8,128)(2,1)S(1)}, bf16[32,64,256]{2,1,0:T(8,128)(2,1)S(1)}, u32[]{:S(2)}, u32[]{:S(2)}) collective-permute-start(bf16[32,64,256]{2,1,0:T(8,128)(2,1)S(1)} %get-tuple-element.55.refs_8_.refs_12_), channel_id=1, source_target_pairs={{0,4},{1,5},{2,6},{3,7},{4,0},{5,1},{6,2},{7,3},{8,12},{9,13},{10,... | collective-permute-start | bytes 3145736 | tf_op jit(solution)/shard_map/ppermute | solution.py:183
  48.6 26.7 %collective-permute-start.6 = (bf16[32,64,256]{2,1,0:T(8,128)(2,1)S(1)}, bf16[32,64,256]{2,1,0:T(8,128)(2,1)S(1)}, u32[]{:S(2)}, u32[]{:S(2)}) collective-permute-start(bf16[32,64,256]{2,1,0:T(8,128)(2,1)S(1)} %select_select_fusion.1), channel_id=1, source_target_pairs={{0,8},{1,9},{2,10},{3,11},{4,12},{5,13},{6,14},{7,15},{8,0},{9,1},... | collective-permute-start | bytes 3145736 | tf_op jit(solution)/shard_map/ppermute | solution.py:183
  52.1 23.2 %collective-permute-start.7 = (bf16[32,64,256]{2,1,0:T(8,128)(2,1)}, bf16[32,64,256]{2,1,0:T(8,128)(2,1)S(1)}, u32[]{:S(2)}, u32[]{:S(2)}) collective-permute-start(bf16[32,64,256]{2,1,0:T(8,128)(2,1)} %collective-permute-done.refs_1_), channel_id=1, source_target_pairs={{8,16},{9,17},{10,18},{11,19},{12,20},{13,21},{14,22},{15,23},{16,... | collective-permute-start | bytes 3145736 | tf_op jit(solution)/shard_map/ppermute | solution.py:183
  75.3 32.3 %collective-permute-start.13 = (bf16[3,32,64,256]{3,2,1,0:T(8,128)(2,1)S(1)}, bf16[3,32,64,256]{3,2,1,0:T(8,128)(2,1)S(1)}, u32[]{:S(2)}, u32[]{:S(2)}) collective-permute-start(bf16[3,32,64,256]{3,2,1,0:T(8,128)(2,1)S(1)} %pad_maximum_fusion), channel_id=1, source_target_pairs={{0,1},{1,0},{2,3},{3,2},{4,5},{5,4},{6,7},{7,6},{8,9},{9,8},{10,11... | collective-permute-start | bytes 9437192 | tf_op jit(solution)/shard_map/ppermute | solution.py:183
  75.4 25.7 %collective-permute-start.10 = (bf16[32,64,256]{2,1,0:T(8,128)(2,1)S(1)}, bf16[32,64,256]{2,1,0:T(8,128)(2,1)}, u32[]{:S(2)}, u32[]{:S(2)}) collective-permute-start(bf16[32,64,256]{2,1,0:T(8,128)(2,1)S(1)} %get-tuple-element.62.refs_9_.refs_13_), channel_id=1, source_target_pairs={{0,4},{1,5},{2,6},{3,7},{4,0},{5,1},{6,2},{7,3},{8,12},{9,13},{10,... | collective-permute-start | bytes 3145736 | tf_op jit(solution)/shard_map/ppermute | solution.py:183
  76.9 25.2 %collective-permute-start.11 = (bf16[32,64,256]{2,1,0:T(8,128)(2,1)S(1)}, bf16[32,64,256]{2,1,0:T(8,128)(2,1)S(1)}, u32[]{:S(2)}, u32[]{:S(2)}) collective-permute-start(bf16[32,64,256]{2,1,0:T(8,128)(2,1)S(1)} %collective-permute-done.4.refs_10_.refs_14_), channel_id=1, source_target_pairs={{0,2},{1,3},{2,0},{3,1},{4,6},{5,7},{6,4},{7,5},{8,10},{9,11},{10,... | collective-permute-start | bytes 3145736 | tf_op jit(solution)/shard_map/ppermute | solution.py:183
  77.4 29.1 %collective-permute-start.12 = (bf16[32,64,256]{2,1,0:T(8,128)(2,1)}, bf16[32,64,256]{2,1,0:T(8,128)(2,1)}, u32[]{:S(2)}, u32[]{:S(2)}) collective-permute-start(bf16[32,64,256]{2,1,0:T(8,128)(2,1)} %collective-permute-done.refs_1_), channel_id=1, source_target_pairs={{0,8},{1,9},{2,10},{3,11},{4,12},{5,13},{6,14},{7,15},{8,0},{9,1},... | collective-permute-start | bytes 3145736 | tf_op jit(solution)/shard_map/ppermute | solution.py:183
  81.3 25.3 %collective-permute-start.9 = (bf16[32,64,256]{2,1,0:T(8,128)(2,1)}, bf16[32,64,256]{2,1,0:T(8,128)(2,1)S(1)}, u32[]{:S(2)}, u32[]{:S(2)}) collective-permute-start(bf16[32,64,256]{2,1,0:T(8,128)(2,1)} %collective-permute-done.1.refs_2_), channel_id=1, source_target_pairs={{8,16},{9,17},{10,18},{11,19},{12,20},{13,21},{14,22},{15,23},{16,... | collective-permute-start | bytes 3145736 | tf_op jit(solution)/shard_map/ppermute | solution.py:183
  109.2 32.0 %collective-permute-start.18 = (bf16[2,32,64,256]{3,2,1,0:T(8,128)(2,1)}, bf16[2,32,64,256]{3,2,1,0:T(8,128)(2,1)S(1)}, u32[]{:S(2)}, u32[]{:S(2)}) collective-permute-start(bf16[2,32,64,256]{3,2,1,0:T(8,128)(2,1)} %pad_maximum_fusion.1), channel_id=1, source_target_pairs={{0,1},{1,0},{2,3},{3,2},{4,5},{5,4},{6,7},{7,6},{8,9},{9,8},{10,11... | collective-permute-start | bytes 6291464 | tf_op jit(solution)/shard_map/ppermute | solution.py:183
  109.2 25.9 %collective-permute-start.15 = (bf16[2,16,64,256]{3,2,1,0:T(8,128)(2,1)}, bf16[2,16,64,256]{3,2,1,0:T(8,128)(2,1)}, u32[]{:S(2)}, u32[]{:S(2)}) collective-permute-start(bf16[2,16,64,256]{3,2,1,0:T(8,128)(2,1)} %get-tuple-element.67), channel_id=1, source_target_pairs={{0,4},{1,5},{2,6},{3,7},{4,0},{5,1},{6,2},{7,3},{8,12},{9,13},{10,... | collective-permute-start | bytes 3145736 | tf_op jit(solution)/shard_map/ppermute | solution.py:183
  109.8 27.6 %collective-permute-start.14 = (bf16[32,64,256]{2,1,0:T(8,128)(2,1)}, bf16[32,64,256]{2,1,0:T(8,128)(2,1)}, u32[]{:S(2)}, u32[]{:S(2)}) collective-permute-start(bf16[32,64,256]{2,1,0:T(8,128)(2,1)} %collective-permute-done.12.refs_3_), channel_id=1, source_target_pairs={{8,16},{9,17},{10,18},{11,19},{12,20},{13,21},{14,22},{15,23},{16,... | collective-permute-start | bytes 3145736 | tf_op jit(solution)/shard_map/ppermute | solution.py:183
  111.4 25.9 %collective-permute-start.16 = (bf16[32,64,256]{2,1,0:T(8,128)(2,1)}, bf16[32,64,256]{2,1,0:T(8,128)(2,1)}, u32[]{:S(2)}, u32[]{:S(2)}) collective-permute-start(bf16[32,64,256]{2,1,0:T(8,128)(2,1)} %collective-permute-done.10.refs_11_.refs_15_), channel_id=1, source_target_pairs={{0,2},{1,3},{2,0},{3,1},{4,6},{5,7},{6,4},{7,5},{8,10},{9,11},{10,... | collective-permute-start | bytes 3145736 | tf_op jit(solution)/shard_map/ppermute | solution.py:183
  113.2 28.0 %collective-permute-start.17 = (bf16[32,64,256]{2,1,0:T(8,128)(2,1)}, bf16[32,64,256]{2,1,0:T(8,128)(2,1)}, u32[]{:S(2)}, u32[]{:S(2)}) collective-permute-start(bf16[32,64,256]{2,1,0:T(8,128)(2,1)} %select_select_fusion), channel_id=1, source_target_pairs={{0,8},{1,9},{2,10},{3,11},{4,12},{5,13},{6,14},{7,15},{8,0},{9,1},... | collective-permute-start | bytes 3145736 | tf_op jit(solution)/shard_map/ppermute | solution.py:183
  141.2 24.5 %collective-permute-start.19 = (bf16[2,16,64,256]{3,2,1,0:T(8,128)(2,1)S(1)}, bf16[2,16,64,256]{3,2,1,0:T(8,128)(2,1)S(1)}, u32[]{:S(2)}, u32[]{:S(2)}) collective-permute-start(bf16[2,16,64,256]{3,2,1,0:T(8,128)(2,1)S(1)} %copy-done.61), channel_id=1, source_target_pairs={{0,4},{1,5},{2,6},{3,7},{4,0},{5,1},{6,2},{7,3},{8,12},{9,13},{10,... | collective-permute-start | bytes 3145736 | tf_op jit(solution)/shard_map/ppermute | solution.py:183
  143.1 102.0 %copy-start.17 = (bf16[32,64,256]{2,1,0:T(8,128)(2,1)}, bf16[32,64,256]{2,1,0:T(8,128)(2,1)S(1)}, u32[]{:S(2)}) copy-start(bf16[32,64,256]{2,1,0:T(8,128)(2,1)S(1)} %get-tuple-element.97.refs_13_.refs_17_) | copy-start | bytes 3145732
  143.1 102.0 %copy-start.19 = (bf16[32,64,256]{2,1,0:T(8,128)(2,1)}, bf16[32,64,256]{2,1,0:T(8,128)(2,1)S(1)}, u32[]{:S(2)}) copy-start(bf16[32,64,256]{2,1,0:T(8,128)(2,1)S(1)} %get-tuple-element.98.refs_12_.refs_16_) | copy-start | bytes 3145732
  144.2 22.8 %collective-permute-start.23 = (bf16[32,64,256]{2,1,0:T(8,128)(2,1)}, bf16[32,64,256]{2,1,0:T(8,128)(2,1)S(1)}, u32[]{:S(2)}, u32[]{:S(2)}) collective-permute-start(bf16[32,64,256]{2,1,0:T(8,128)(2,1)} %collective-permute-done.16.refs_19_.refs_23_), channel_id=1, source_target_pairs={{0,1},{1,0},{2,3},{3,2},{4,5},{5,4},{6,7},{7,6},{8,9},{9,8},{10,11... | collective-permute-start | bytes 3145736 | tf_op jit(solution)/shard_map/ppermute | solution.py:183
  151.7 47.6 %collective-permute-start.20 = (bf16[2,16,64,256]{3,2,1,0:T(8,128)(2,1)S(1)}, bf16[2,16,64,256]{3,2,1,0:T(8,128)(2,1)S(1)}, u32[]{:S(2)}, u32[]{:S(2)}) collective-permute-start(bf16[2,16,64,256]{3,2,1,0:T(8,128)(2,1)S(1)} %pad_maximum_fusion.6.refs_0_.refs_1_), channel_id=1, source_target_pairs={{0,8},{1,9},{2,10},{3,11},{4,12},{5,13},{6,14},{7,15},{8,0},{9,1},... | collective-permute-start | bytes 3145736 | tf_op jit(solution)/shard_map/ppermute | solution.py:183
  153.5 45.8 %collective-permute-start.21 = (bf16[2,16,64,256]{3,2,1,0:T(8,128)(2,1)S(1)}, bf16[2,16,64,256]{3,2,1,0:T(8,128)(2,1)S(1)}, u32[]{:S(2)}, u32[]{:S(2)}) collective-permute-start(bf16[2,16,64,256]{3,2,1,0:T(8,128)(2,1)S(1)} %pad_maximum_fusion.6.refs_0_.refs_1_), channel_id=1, source_target_pairs={{8,16},{9,17},{10,18},{11,19},{12,20},{13,21},{14,22},{15,23},{16,... | collective-permute-start | bytes 3145736 | tf_op jit(solution)/shard_map/ppermute | solution.py:183
  154.2 45.1 %collective-permute-start.22 = (bf16[32,64,256]{2,1,0:T(8,128)(2,1)S(1)}, bf16[32,64,256]{2,1,0:T(8,128)(2,1)S(1)}, u32[]{:S(2)}, u32[]{:S(2)}) collective-permute-start(bf16[32,64,256]{2,1,0:T(8,128)(2,1)S(1)} %copy-done.7), channel_id=1, source_target_pairs={{8,10},{9,11},{10,8},{11,9},{12,14},{13,15},{14,12},{15,13},{16,18... | collective-permute-start | bytes 3145736 | tf_op jit(solution)/shard_map/ppermute | solution.py:183
  167.0 39.4 %copy-start.25 = (bf16[32,64,256]{2,1,0:T(8,128)(2,1)}, bf16[32,64,256]{2,1,0:T(8,128)(2,1)S(1)}, u32[]{:S(2)}) copy-start(bf16[32,64,256]{2,1,0:T(8,128)(2,1)S(1)} %collective-permute-done.23.refs_23_.refs_27_) | copy-start | bytes 3145732
  167.1 39.3 %copy-start.38 = (bf16[2,16,64,256]{3,2,1,0:T(8,128)(2,1)S(1)}, bf16[2,16,64,256]{3,2,1,0:T(8,128)(2,1)}, u32[]{:S(2)}) copy-start(bf16[2,16,64,256]{3,2,1,0:T(8,128)(2,1)} %copy-done.37) | copy-start | bytes 3145732
  199.3 39.4 %copy-start.21 = (bf16[32,64,256]{2,1,0:T(8,128)(2,1)}, bf16[32,64,256]{2,1,0:T(8,128)(2,1)S(1)}, u32[]{:S(2)}) copy-start(bf16[32,64,256]{2,1,0:T(8,128)(2,1)S(1)} %collective-permute-done.22.refs_5_) | copy-start | bytes 3145732
  199.3 39.4 %collective-permute-start.27 = (bf16[32,64,256]{2,1,0:T(8,128)(2,1)}, bf16[32,64,256]{2,1,0:T(8,128)(2,1)S(1)}, u32[]{:S(2)}, u32[]{:S(2)}) collective-permute-start(bf16[32,64,256]{2,1,0:T(8,128)(2,1)} %collective-permute-done.17.refs_6_), channel_id=1, source_target_pairs={{8,10},{9,11},{10,8},{11,9},{12,14},{13,15},{14,12},{15,13},{16,18... | collective-permute-start | bytes 3145736 | tf_op jit(solution)/shard_map/ppermute | solution.py:183
  200.2 39.6 %collective-permute-start.28 = (bf16[2,32,64,256]{3,2,1,0:T(8,128)(2,1)}, bf16[2,32,64,256]{3,2,1,0:T(8,128)(2,1)}, u32[]{:S(2)}, u32[]{:S(2)}) collective-permute-start(bf16[2,32,64,256]{3,2,1,0:T(8,128)(2,1)} %pad_maximum_fusion.2), channel_id=1, source_target_pairs={{0,1},{1,0},{2,3},{3,2},{4,5},{5,4},{6,7},{7,6},{8,9},{9,8},{10,11... | collective-permute-start | bytes 6291464 | tf_op jit(solution)/shard_map/ppermute | solution.py:183
  200.2 39.5 %collective-permute-start.24 = (bf16[32,64,256]{2,1,0:T(8,128)(2,1)}, bf16[32,64,256]{2,1,0:T(8,128)(2,1)S(1)}, u32[]{:S(2)}, u32[]{:S(2)}) collective-permute-start(bf16[32,64,256]{2,1,0:T(8,128)(2,1)} %get-tuple-element.76), channel_id=1, source_target_pairs={{0,4},{1,5},{2,6},{3,7},{4,0},{5,1},{6,2},{7,3},{8,12},{9,13},{10,... | collective-permute-start | bytes 3145736 | tf_op jit(solution)/shard_map/ppermute | solution.py:183
  201.8 37.9 %collective-permute-start.25 = (bf16[2,16,64,256]{3,2,1,0:T(8,128)(2,1)S(1)}, bf16[2,16,64,256]{3,2,1,0:T(8,128)(2,1)}, u32[]{:S(2)}, u32[]{:S(2)}) collective-permute-start(bf16[2,16,64,256]{3,2,1,0:T(8,128)(2,1)S(1)} %pad_maximum_fusion.7.refs_0_.refs_1_), channel_id=1, source_target_pairs={{0,8},{1,9},{2,10},{3,11},{4,12},{5,13},{6,14},{7,15},{8,0},{9,1},... | collective-permute-start | bytes 3145736 | tf_op jit(solution)/shard_map/ppermute | solution.py:183
  205.7 34.0 %collective-permute-start.26 = (bf16[2,16,64,256]{3,2,1,0:T(8,128)(2,1)S(1)}, bf16[2,16,64,256]{3,2,1,0:T(8,128)(2,1)S(1)}, u32[]{:S(2)}, u32[]{:S(2)}) collective-permute-start(bf16[2,16,64,256]{3,2,1,0:T(8,128)(2,1)S(1)} %collective-permute-done.20.refs_2_.refs_3_), channel_id=1, source_target_pairs={{8,16},{9,17},{10,18},{11,19},{12,20},{13,21},{14,22},{15,23},{16,... | collective-permute-start | bytes 3145736 | tf_op jit(solution)/shard_map/ppermute | solution.py:183
  242.5 33.6 %collective-permute-start.30 = (bf16[2,16,64,256]{3,2,1,0:T(8,128)(2,1)}, bf16[2,16,64,256]{3,2,1,0:T(8,128)(2,1)}, u32[]{:S(2)}, u32[]{:S(2)}) collective-permute-start(bf16[2,16,64,256]{3,2,1,0:T(8,128)(2,1)} %maximum_select_fusion), channel_id=1, source_target_pairs={{0,8},{1,9},{2,10},{3,11},{4,12},{5,13},{6,14},{7,15},{8,0},{9,1},... | collective-permute-start | bytes 3145736 | tf_op jit(solution)/shard_map/ppermute | solution.py:183
  244.3 33.6 %collective-permute-start.31 = (bf16[2,32,64,256]{3,2,1,0:T(8,128)(2,1)S(1)}, bf16[2,32,64,256]{3,2,1,0:T(8,128)(2,1)S(1)}, u32[]{:S(2)}, u32[]{:S(2)}) collective-permute-start(bf16[2,32,64,256]{3,2,1,0:T(8,128)(2,1)S(1)} %pad_maximum_fusion.3), channel_id=1, source_target_pairs={{0,1},{1,0},{2,3},{3,2},{4,5},{5,4},{6,7},{7,6},{8,9},{9,8},{10,11... | collective-permute-start | bytes 6291464 | tf_op jit(solution)/shard_map/ppermute | solution.py:183
  244.3 33.6 %collective-permute-start.29 = (bf16[2,16,64,256]{3,2,1,0:T(8,128)(2,1)S(1)}, bf16[2,16,64,256]{3,2,1,0:T(8,128)(2,1)S(1)}, u32[]{:S(2)}, u32[]{:S(2)}) collective-permute-start(bf16[2,16,64,256]{3,2,1,0:T(8,128)(2,1)S(1)} %pad_maximum_fusion.7.refs_0_.refs_1_), channel_id=1, source_target_pairs={{8,16},{9,17},{10,18},{11,19},{12,20},{13,21},{14,22},{15,23},{16,... | collective-permute-start | bytes 3145736 | tf_op jit(solution)/shard_map/ppermute | solution.py:183
  277.9 25.8 %collective-permute-start.32 = (bf16[2,16,64,256]{3,2,1,0:T(8,128)(2,1)}, bf16[2,16,64,256]{3,2,1,0:T(8,128)(2,1)S(1)}, u32[]{:S(2)}, u32[]{:S(2)}) collective-permute-start(bf16[2,16,64,256]{3,2,1,0:T(8,128)(2,1)} %collective-permute-done.25.refs_2_.refs_3_), channel_id=1, source_target_pairs={{8,16},{9,17},{10,18},{11,19},{12,20},{13,21},{14,22},{15,23},{16,... | collective-permute-start | bytes 3145736 | tf_op jit(solution)/shard_map/ppermute | solution.py:183
  279.0 28.3 %collective-permute-start.33 = (bf16[2,16,64,256]{3,2,1,0:T(8,128)(2,1)}, bf16[2,16,64,256]{3,2,1,0:T(8,128)(2,1)S(1)}, u32[]{:S(2)}, u32[]{:S(2)}) collective-permute-start(bf16[2,16,64,256]{3,2,1,0:T(8,128)(2,1)} %maximum_select_fusion.2), channel_id=1, source_target_pairs={{0,8},{1,9},{2,10},{3,11},{4,12},{5,13},{6,14},{7,15},{8,0},{9,1},... | collective-permute-start | bytes 3145736 | tf_op jit(solution)/shard_map/ppermute | solution.py:183
  357.6 2.9 collective-permute-start.34
  363.3 8.4 %collective-permute-start.37 = (f32[2,4,16,512]{3,2,1,0:T(8,128)S(1)}, f32[2,4,16,512]{3,2,1,0:T(8,128)S(1)}, u32[]{:S(2)}, u32[]{:S(2)}) collective-permute-start(f32[2,4,16,512]{3,2,1,0:T(8,128)S(1)} %bitcast.146), channel_id=1, source_target_pairs={{0,2},{1,3},{2,0},{3,1},{4,6},{5,7},{6,4},{7,5},{8,10},{9,11},{10,... | collective-permute-start | bytes 786440 | tf_op jit(solution)/shard_map/ppermute | solution.py:183
  364.9 8.1 %collective-permute-start.35 = (f32[2,4,16,512]{3,2,1,0:T(8,128)S(1)}, f32[2,4,16,512]{3,2,1,0:T(8,128)S(1)}, u32[]{:S(2)}, u32[]{:S(2)}) collective-permute-start(f32[2,4,16,512]{3,2,1,0:T(8,128)S(1)} %dynamic-slice_bitcast_fusion.5), channel_id=1, source_target_pairs={{0,4},{1,5},{2,6},{3,7},{4,0},{5,1},{6,2},{7,3},{8,12},{9,13},{10,... | collective-permute-start | bytes 786440 | tf_op jit(solution)/shard_map/ppermute | solution.py:183
  371.8 5.0 %collective-permute-start.38 = (f32[4,16,512]{2,1,0:T(8,128)S(1)}, f32[4,16,512]{2,1,0:T(8,128)S(1)}, u32[]{:S(2)}, u32[]{:S(2)}) collective-permute-start(f32[4,16,512]{2,1,0:T(8,128)S(1)} %dynamic-slice_bitcast_fusion.6), channel_id=1, source_target_pairs={{0,4},{1,5},{2,6},{3,7},{4,0},{5,1},{6,2},{7,3},{8,12},{9,13},{10,... | collective-permute-start | bytes 393224 | tf_op jit(solution)/shard_map/ppermute | solution.py:183
  373.1 5.0 %collective-permute-start.36 = (f32[4,16,512]{2,1,0:T(8,128)S(1)}, f32[4,16,512]{2,1,0:T(8,128)S(1)}, u32[]{:S(2)}, u32[]{:S(2)}) collective-permute-start(f32[4,16,512]{2,1,0:T(8,128)S(1)} %dynamic-slice_bitcast_fusion.7), channel_id=1, source_target_pairs={{0,2},{1,3},{2,0},{3,1},{4,6},{5,7},{6,4},{7,5},{8,10},{9,11},{10,... | collective-permute-start | bytes 393224 | tf_op jit(solution)/shard_map/ppermute | solution.py:183
  378.2 5.2 %collective-permute-start.39 = (f32[32,512]{1,0:T(8,128)S(1)}, f32[32,512]{1,0:T(8,128)S(1)}, u32[]{:S(2)}, u32[]{:S(2)}) collective-permute-start(f32[32,512]{1,0:T(8,128)S(1)} %get-tuple-element.133), channel_id=1, source_target_pairs={{0,8},{1,9},{2,10},{3,11},{4,12},{5,13},{6,14},{7,15},{8,0},{9,1},... | collective-permute-start | bytes 196616 | tf_op jit(solution)/shard_map/ppermute | solution.py:183
  379.5 5.9 %collective-permute-start.40 = (f32[32,512]{1,0:T(8,128)S(1)}, f32[32,512]{1,0:T(8,128)S(1)}, u32[]{:S(2)}, u32[]{:S(2)}) collective-permute-start(f32[32,512]{1,0:T(8,128)S(1)} %get-tuple-element.134), channel_id=1, source_target_pairs={{0,16},{1,17},{2,18},{3,19},{4,20},{5,21},{6,22},{7,23},{8,24},{9,... | collective-permute-start | bytes 196616 | tf_op jit(solution)/shard_map/ppermute | solution.py:183
  380.5 6.2 %collective-permute-start.41 = (f32[32,512]{1,0:T(8,128)S(1)}, f32[32,512]{1,0:T(8,128)S(1)}, u32[]{:S(2)}, u32[]{:S(2)}) collective-permute-start(f32[32,512]{1,0:T(8,128)S(1)} %get-tuple-element.135), channel_id=1, source_target_pairs={{0,24},{1,25},{2,26},{3,27},{4,28},{5,29},{6,30},{7,31},{8,16},{9,... | collective-permute-start | bytes 196616 | tf_op jit(solution)/shard_map/ppermute | solution.py:183
  (59 other events, 809.0 us)
